TPU v7x, 256 devices: a whole 4x4x8 slice. The times are simulated.
256 devices in a mesh: rows: 64 (over y, z, core), dp: 4 (over x).
Axes of the slice: x: 4, y: 4, z: 8, core: 2. Of those that a mesh axis runs over, the one named last changes fastest.
Arguments:
- tokens: bfloat16 [4, 1024, 128, 256], P('dp', 'rows'), may hold values from -6 to 6
- norm_gain: float32 [256], replicated, may hold values from 0.1 to 1.9
- in_weight: bfloat16 [256, 768], replicated, may hold values from -16 to 16
- out_weight: bfloat16 [256, 256], replicated, may hold values from -0.375 to 0.375
- cotangent: bfloat16 [4, 1024, 128, 256], P('dp', 'rows'), may hold values from -6 to 6
Outputs:
- grad_tokens: bfloat16 [4, 1024, 128, 256], P('dp', 'rows')
- grad_in_weight: float32 [256, 768], replicated
- grad_out_weight: float32 [256, 256], replicated
- grad_gain: float32 [256], replicated
All inputs are finite; a program needn't handle non-finite values.
Results may differ from a plain program's by a relative error of at most 0.011.
Values may be sent and summed in bfloat16 or wider, within the bound.
A program may use at most 128 MiB of HBM per device.

v0:
```python
import math

import jax
import jax.numpy as jnp
from jax import lax
from jax.sharding import PartitionSpec as P


def with_halo(cells, sides, width):
    for axis, dim in sides:
        count = lax.axis_size(axis)
        ends = count - 1
        head = lax.slice_in_dim(cells, 0, width, axis=dim)
        tail = lax.slice_in_dim(cells, cells.shape[dim] - width, cells.shape[dim], axis=dim)
        cells = jnp.concatenate(
            [
                lax.ppermute(tail, axis, [(i, (i + 1) % count) for i in range(ends)]),
                cells,
                lax.ppermute(head, axis, [((i + 1) % count, i) for i in range(ends)]),
            ],
            axis=dim,
        )
    return cells


def to_query_tiles(field, tile_cols):
    rows_here, columns, channels = field.shape
    tile_count = columns // tile_cols
    shaped = field.reshape(rows_here, tile_count, tile_cols, channels)
    return jnp.transpose(shaped, (1, 0, 2, 3)).reshape(tile_count, rows_here * tile_cols, channels)


def from_query_tiles(tile_set, rows_here):
    tile_count, query_rows, channels = tile_set.shape
    tile_cols = query_rows // rows_here
    shaped = tile_set.reshape(tile_count, rows_here, tile_cols, channels)
    return jnp.transpose(shaped, (1, 0, 2, 3)).reshape(rows_here, tile_count * tile_cols, channels)


def to_key_tiles(extended, tile_cols):
    frame_rows, columns, channels = extended.shape
    tile_count = columns // tile_cols
    key_frame = jnp.pad(extended, ((0, 0), (3, tile_cols - 3), (0, 0)))
    main_part = key_frame[:, :columns].reshape(frame_rows, tile_count, tile_cols, channels)
    spill_over = key_frame[:, tile_cols:].reshape(frame_rows, tile_count, tile_cols, channels)[
        :, :, :6
    ]
    joined = jnp.concatenate([main_part, spill_over], axis=2)
    return jnp.transpose(joined, (1, 0, 2, 3)).reshape(
        tile_count, frame_rows * (tile_cols + 6), channels
    )


def from_key_tiles(tile_set, frame_rows, tile_cols):
    tile_count = tile_set.shape[0]
    channels = tile_set.shape[2]
    columns = tile_count * tile_cols
    shaped = jnp.transpose(
        tile_set.reshape(tile_count, frame_rows, tile_cols + 6, channels), (1, 0, 2, 3)
    )
    main_part = shaped[:, :, :tile_cols].reshape(frame_rows, columns, channels)
    spill_over = jnp.pad(
        shaped[:, :, tile_cols:], ((0, 0), (0, 0), (0, tile_cols - 6), (0, 0))
    ).reshape(frame_rows, columns, channels)
    framed = jnp.pad(main_part, ((0, 0), (0, tile_cols), (0, 0))) + jnp.pad(
        spill_over, ((0, 0), (tile_cols, 0), (0, 0))
    )
    return framed[:, 3 : 3 + columns]


def tile_masks(rows_here, columns, tile_cols, first_row, all_rows):
    tile_count = columns // tile_cols
    key_width = tile_cols + 6
    key_index = jnp.arange((rows_here + 6) * key_width)
    key_row = key_index // key_width
    key_col = key_index % key_width
    query_index = jnp.arange(rows_here * tile_cols)
    query_row = query_index // tile_cols
    query_col = query_index % tile_cols
    near = (jnp.abs(key_row[:, None] - 3 - query_row[None, :]) <= 3) & (
        jnp.abs(key_col[:, None] - 3 - query_col[None, :]) <= 3
    )
    global_row = first_row + key_row - 3
    row_inside = (global_row >= 0) & (global_row < all_rows)
    global_col = jnp.arange(tile_count)[:, None] * tile_cols + key_col[None, :] - 3
    col_inside = (global_col >= 0) & (global_col < columns)
    return near[None] & row_inside[None, :, None] & col_inside[:, :, None]


def by_groups(step_fn, operands, group_size):
    shaped = tuple(
        (
            member.reshape((member.shape[0] // group_size, group_size) + member.shape[1:])
            for member in operands
        )
    )
    results = lax.map(step_fn, shaped)
    return tuple(
        (
            member.reshape((member.shape[0] * member.shape[1],) + member.shape[2:])
            for member in results
        )
    )


def query_side(operands):
    queries, keys, values, upstream, allowed = operands
    group_size, query_rows, model_width = queries.shape
    key_rows = keys.shape[1]
    head_count = model_width // 64
    query_heads = queries.reshape(group_size, query_rows, head_count, 64)
    key_heads = keys.reshape(group_size, key_rows, head_count, 64)
    value_heads = values.reshape(group_size, key_rows, head_count, 64)
    up_heads = upstream.reshape(group_size, query_rows, head_count, 64)
    scores = (
        jnp.einsum("tqhe,tkhe->thkq", query_heads, key_heads, preferred_element_type=jnp.float32)
        * 0.125
    )
    scores = jnp.where(allowed[:, None], scores, -jnp.inf)
    row_max = jnp.max(scores, axis=2, keepdims=True)
    log_total = row_max + jnp.log(jnp.sum(jnp.exp(scores - row_max), axis=2, keepdims=True))
    probability = jnp.exp(scores - log_total)
    weights = probability.astype(jnp.bfloat16)
    attended = jnp.einsum(
        "thkq,tkhe->tqhe", weights, value_heads, preferred_element_type=jnp.float32
    )
    attended = attended.astype(jnp.bfloat16).reshape(group_size, query_rows, model_width)
    grad_prob = jnp.einsum(
        "tqhe,tkhe->thkq", up_heads, value_heads, preferred_element_type=jnp.float32
    )
    delta_sum = jnp.sum(probability * grad_prob, axis=2, keepdims=True)
    grad_score = (probability * (grad_prob - delta_sum) * 0.125).astype(jnp.bfloat16)
    grad_query = jnp.einsum(
        "thkq,tkhe->tqhe", grad_score, key_heads, preferred_element_type=jnp.float32
    )
    results = (
        attended,
        grad_query.reshape(group_size, query_rows, model_width),
        log_total[:, :, 0],
        delta_sum[:, :, 0],
    )
    grad_key = jnp.einsum(
        "thkq,tqhe->tkhe", grad_score, query_heads, preferred_element_type=jnp.float32
    )
    grad_value = jnp.einsum(
        "thkq,tqhe->tkhe", weights, up_heads, preferred_element_type=jnp.float32
    )
    results = results + (
        grad_key.reshape(group_size, key_rows, model_width),
        grad_value.reshape(group_size, key_rows, model_width),
    )
    return results


def local(tokens, norm_gain, in_weight, out_weight, cotangent):
    rows_here, columns, model_width = (tokens.shape[1], tokens.shape[2], tokens.shape[3])
    tile_cols = 32
    tile_count = columns // tile_cols
    query_rows = rows_here * tile_cols
    group_size = tile_count
    for candidate in range(tile_count, 0, -1):
        if tile_count % candidate == 0 and candidate * query_rows >= 512:
            group_size = candidate
    wide_input = tokens[0].astype(jnp.float32)
    inv_rms = lax.rsqrt(jnp.mean(wide_input * wide_input, axis=-1, keepdims=True) + 1e-06)
    normed = (wide_input * inv_rms * norm_gain).astype(jnp.bfloat16)
    flat_norm = normed.reshape(-1, model_width)
    projected = jnp.dot(flat_norm, in_weight, preferred_element_type=jnp.float32).astype(
        jnp.bfloat16
    )
    projected = projected.reshape(rows_here, columns, 3 * model_width)
    flat_up = cotangent[0].reshape(-1, model_width)
    grad_attn = lax.dot_general(
        flat_up, out_weight, (((1,), (1,)), ((), ())), preferred_element_type=jnp.float32
    )
    grad_attn = grad_attn.astype(jnp.bfloat16).reshape(rows_here, columns, model_width)
    first_row = lax.axis_index("rows") * rows_here
    all_rows = lax.axis_size("rows") * rows_here
    allowed = tile_masks(rows_here, columns, tile_cols, first_row, all_rows)
    query_tiles = to_query_tiles(projected[:, :, :model_width], tile_cols)
    up_tiles = to_query_tiles(grad_attn, tile_cols)
    extended = with_halo(projected[:, :, model_width:], (("rows", 0),), 3)
    near_tiles = to_key_tiles(extended, tile_cols)
    attended, grad_query, log_total, delta_sum, grad_key_tiles, grad_value_tiles = by_groups(
        lambda operands: query_side(operands),
        (
            query_tiles,
            near_tiles[:, :, :model_width],
            near_tiles[:, :, model_width:],
            up_tiles,
            allowed,
        ),
        group_size,
    )
    key_frame = from_key_tiles(grad_key_tiles, rows_here + 6, tile_cols)
    value_frame = from_key_tiles(grad_value_tiles, rows_here + 6, tile_cols)
    rim_keys = jnp.concatenate([key_frame[:3], key_frame[-3:]], axis=0)
    rim_values = jnp.concatenate([value_frame[:3], value_frame[-3:]], axis=0)
    received_key, received_value = (
        with_halo(rim_keys.astype(jnp.bfloat16), (("rows", 0),), 3).astype(rim_keys.dtype),
        with_halo(rim_values.astype(jnp.bfloat16), (("rows", 0),), 3).astype(rim_values.dtype),
    )
    grad_key = (
        key_frame[3 : 3 + rows_here].at[:3].add(received_key[:3]).at[-3:].add(received_key[-3:])
    )
    grad_value = (
        value_frame[3 : 3 + rows_here]
        .at[:3]
        .add(received_value[:3])
        .at[-3:]
        .add(received_value[-3:])
    )
    grad_query = from_query_tiles(grad_query, rows_here)
    attended = from_query_tiles(attended, rows_here)
    joined = jnp.concatenate([grad_query, grad_key, grad_value], axis=-1).astype(jnp.bfloat16)
    flat_joined = joined.reshape(-1, 3 * model_width)
    grad_in_weight = lax.dot_general(
        flat_norm, flat_joined, (((0,), (0,)), ((), ())), preferred_element_type=jnp.float32
    )
    grad_out_weight = lax.dot_general(
        attended.reshape(-1, model_width),
        flat_up,
        (((0,), (0,)), ((), ())),
        preferred_element_type=jnp.float32,
    )
    grad_normed = lax.dot_general(
        flat_joined, in_weight, (((1,), (1,)), ((), ())), preferred_element_type=jnp.float32
    )
    grad_normed = grad_normed.reshape(rows_here, columns, model_width)
    grad_gain = jnp.sum(grad_normed * wide_input * inv_rms, axis=(0, 1))
    grad_in_weight, grad_out_weight, grad_gain = lax.psum(
        (grad_in_weight, grad_out_weight, grad_gain), ("rows", "dp")
    )
    factor = 1.0 / math.sqrt(lax.axis_size("rows") * lax.axis_size("dp") * rows_here * columns)
    gained = grad_normed * norm_gain
    grad_tokens = (
        inv_rms
        * (
            gained
            - wide_input * inv_rms * inv_rms * jnp.mean(gained * wide_input, axis=-1, keepdims=True)
        )
    ).astype(jnp.bfloat16)
    return (
        grad_tokens[None],
        grad_in_weight * factor,
        grad_out_weight * factor,
        grad_gain * factor,
    )


def solution(mesh):
    return jax.shard_map(
        local,
        mesh=mesh,
        in_specs=(P("dp", "rows", None, None), P(), P(), P(), P("dp", "rows", None, None)),
        out_specs=(P("dp", "rows", None, None), P(), P(), P()),
        check_vma=False,
    )
```

profile of v0, /device:TPU:1, one launch (start us, length us, event | category | flops | bytes accessed | tf_op | source)
XLA Modules:
  0.0 781.5 jit_solution(5211280555520209158)
XLA Ops:
  14.7 4.9 collective-permute-start
  50.6 351.3 %while.20 = (s32[]{:T(128)}, bf16[4,1,512,256]{3,2,0,1:T(8,128)(2,1)}, bf16[4,1,512,256]{3,2,0,1:T(8,128)(2,1)}, f32[4,1,836,256]{3,0,2,1:T(4,128)}, f32[4,1,836...) while((s32[]{:T(128)}, ...), condition=%wide.region_5.6_spmd, body=%wide.region_1.5_spmd.sunk | while | flops 1378397824 | bytes 110289064 | solution.py:97
  66.3 11.2 %fusion.151 = bf16[4,64,512]{2,1,0:T(8,128)(2,1)S(1)} fusion(bf16[836,4,64]{0,2,1:T(8,128)(2,1)S(1)} %bitcast.173, f32[4,836,512]{2,1,0:T(8,128)} %fusion.149, f32[4,836,512]{2,1,0:T(8,128)} %copy-done.1, f32[4,512]{1,0:T(4,128)S(1)} %log_add_fusion.2, pred[836,512]{1,0:T(8,128)(4,1)S(1)} %dynamic-slice_bitcast_fusion.2), kind=kOutput, calls=%fused_computation.10.clone.1 | convolution fusion | flops 237988672 | bytes 14823424 | tf_op jit(solution)/shard_map/while/body/eval_jaxpr/thkq,tkhe->tqhe/dot_general | solution.py:133
  77.5 12.2 %fusion.152 = f32[4,64,836]{2,1,0:T(8,128)} fusion(bf16[512,4,64]{0,2,1:T(8,128)(2,1)S(1)} %bitcast.180, f32[4,836,512]{2,1,0:T(8,128)} %fusion.149, f32[4,836,512]{2,1,0:T(8,128)} %copy-done.1, f32[4,512]{1,0:T(4,128)S(1)} %log_add_fusion.2, pred[836,512]{1,0:T(8,128)(4,1)S(1)} %dynamic-slice_bitcast_fusion.2), kind=kOutput, calls=%fused_computation.9.clone.1 | convolution fusion | flops 237988672 | bytes 15251456 | tf_op jit(solution)/shard_map/while/body/eval_jaxpr/thkq,tqhe->tkhe/dot_general | solution.py:142
  89.7 4.8 fusion.153
  99.4 19.5 %dynamic_update_slice.21 = f32[4,1,836,256]{3,0,2,1:T(4,128)} dynamic-update-slice(f32[4,1,836,256]{3,0,2,1:T(4,128)} %get-tuple-element.260, f32[1,1,836,256]{3,0,2,1:T(1,128)S(1)} %copy.84, s32[]{:T(128)S(6)} %copy.95, s32[]{:T(128)} %constant.195.clone.1..sunk, s32[]{:T(128)} %constant.195.clone.1..sunk, s32[]{:T(128)} %constant.195.clone.1..sunk) | dynamic-update-slice | bytes 1712132 | tf_op jit(solution)/shard_map/while/body/jit(dynamic_update_index_in_dim)/dynamic_update_slice | solution.py:97
  118.9 19.5 %dynamic_update_slice.22 = f32[4,1,836,256]{3,0,2,1:T(4,128)} dynamic-update-slice(f32[4,1,836,256]{3,0,2,1:T(4,128)} %get-tuple-element.261, f32[1,1,836,256]{3,0,2,1:T(1,128)S(1)} %copy.85, s32[]{:T(128)S(6)} %copy.95, s32[]{:T(128)} %constant.195.clone.1..sunk, s32[]{:T(128)} %constant.195.clone.1..sunk, s32[]{:T(128)} %constant.195.clone.1..sunk) | dynamic-update-slice | bytes 1712132 | tf_op jit(solution)/shard_map/while/body/jit(dynamic_update_index_in_dim)/dynamic_update_slice | solution.py:97
  154.1 11.2 %fusion.151 = bf16[4,64,512]{2,1,0:T(8,128)(2,1)S(1)} fusion(bf16[836,4,64]{0,2,1:T(8,128)(2,1)S(1)} %bitcast.173, f32[4,836,512]{2,1,0:T(8,128)} %fusion.149, f32[4,836,512]{2,1,0:T(8,128)} %copy-done.1, f32[4,512]{1,0:T(4,128)S(1)} %log_add_fusion.2, pred[836,512]{1,0:T(8,128)(4,1)S(1)} %dynamic-slice_bitcast_fusion.2), kind=kOutput, calls=%fused_computation.10.clone.1 | convolution fusion | flops 237988672 | bytes 14823424 | tf_op jit(solution)/shard_map/while/body/eval_jaxpr/thkq,tkhe->tqhe/dot_general | solution.py:133
  165.3 12.2 %fusion.152 = f32[4,64,836]{2,1,0:T(8,128)} fusion(bf16[512,4,64]{0,2,1:T(8,128)(2,1)S(1)} %bitcast.180, f32[4,836,512]{2,1,0:T(8,128)} %fusion.149, f32[4,836,512]{2,1,0:T(8,128)} %copy-done.1, f32[4,512]{1,0:T(4,128)S(1)} %log_add_fusion.2, pred[836,512]{1,0:T(8,128)(4,1)S(1)} %dynamic-slice_bitcast_fusion.2), kind=kOutput, calls=%fused_computation.9.clone.1 | convolution fusion | flops 237988672 | bytes 15251456 | tf_op jit(solution)/shard_map/while/body/eval_jaxpr/thkq,tqhe->tkhe/dot_general | solution.py:142
  177.6 4.8 fusion.153
  187.3 19.5 %dynamic_update_slice.21 = f32[4,1,836,256]{3,0,2,1:T(4,128)} dynamic-update-slice(f32[4,1,836,256]{3,0,2,1:T(4,128)} %get-tuple-element.260, f32[1,1,836,256]{3,0,2,1:T(1,128)S(1)} %copy.84, s32[]{:T(128)S(6)} %copy.95, s32[]{:T(128)} %constant.195.clone.1..sunk, s32[]{:T(128)} %constant.195.clone.1..sunk, s32[]{:T(128)} %constant.195.clone.1..sunk) | dynamic-update-slice | bytes 1712132 | tf_op jit(solution)/shard_map/while/body/jit(dynamic_update_index_in_dim)/dynamic_update_slice | solution.py:97
  206.8 19.5 %dynamic_update_slice.22 = f32[4,1,836,256]{3,0,2,1:T(4,128)} dynamic-update-slice(f32[4,1,836,256]{3,0,2,1:T(4,128)} %get-tuple-element.261, f32[1,1,836,256]{3,0,2,1:T(1,128)S(1)} %copy.85, s32[]{:T(128)S(6)} %copy.95, s32[]{:T(128)} %constant.195.clone.1..sunk, s32[]{:T(128)} %constant.195.clone.1..sunk, s32[]{:T(128)} %constant.195.clone.1..sunk) | dynamic-update-slice | bytes 1712132 | tf_op jit(solution)/shard_map/while/body/jit(dynamic_update_index_in_dim)/dynamic_update_slice | solution.py:97
  242.0 11.2 %fusion.151 = bf16[4,64,512]{2,1,0:T(8,128)(2,1)S(1)} fusion(bf16[836,4,64]{0,2,1:T(8,128)(2,1)S(1)} %bitcast.173, f32[4,836,512]{2,1,0:T(8,128)} %fusion.149, f32[4,836,512]{2,1,0:T(8,128)} %copy-done.1, f32[4,512]{1,0:T(4,128)S(1)} %log_add_fusion.2, pred[836,512]{1,0:T(8,128)(4,1)S(1)} %dynamic-slice_bitcast_fusion.2), kind=kOutput, calls=%fused_computation.10.clone.1 | convolution fusion | flops 237988672 | bytes 14823424 | tf_op jit(solution)/shard_map/while/body/eval_jaxpr/thkq,tkhe->tqhe/dot_general | solution.py:133
  253.2 12.2 %fusion.152 = f32[4,64,836]{2,1,0:T(8,128)} fusion(bf16[512,4,64]{0,2,1:T(8,128)(2,1)S(1)} %bitcast.180, f32[4,836,512]{2,1,0:T(8,128)} %fusion.149, f32[4,836,512]{2,1,0:T(8,128)} %copy-done.1, f32[4,512]{1,0:T(4,128)S(1)} %log_add_fusion.2, pred[836,512]{1,0:T(8,128)(4,1)S(1)} %dynamic-slice_bitcast_fusion.2), kind=kOutput, calls=%fused_computation.9.clone.1 | convolution fusion | flops 237988672 | bytes 15251456 | tf_op jit(solution)/shard_map/while/body/eval_jaxpr/thkq,tqhe->tkhe/dot_general | solution.py:142
  265.4 4.8 fusion.153
  275.1 19.5 %dynamic_update_slice.21 = f32[4,1,836,256]{3,0,2,1:T(4,128)} dynamic-update-slice(f32[4,1,836,256]{3,0,2,1:T(4,128)} %get-tuple-element.260, f32[1,1,836,256]{3,0,2,1:T(1,128)S(1)} %copy.84, s32[]{:T(128)S(6)} %copy.95, s32[]{:T(128)} %constant.195.clone.1..sunk, s32[]{:T(128)} %constant.195.clone.1..sunk, s32[]{:T(128)} %constant.195.clone.1..sunk) | dynamic-update-slice | bytes 1712132 | tf_op jit(solution)/shard_map/while/body/jit(dynamic_update_index_in_dim)/dynamic_update_slice | solution.py:97
  294.6 19.5 %dynamic_update_slice.22 = f32[4,1,836,256]{3,0,2,1:T(4,128)} dynamic-update-slice(f32[4,1,836,256]{3,0,2,1:T(4,128)} %get-tuple-element.261, f32[1,1,836,256]{3,0,2,1:T(1,128)S(1)} %copy.85, s32[]{:T(128)S(6)} %copy.95, s32[]{:T(128)} %constant.195.clone.1..sunk, s32[]{:T(128)} %constant.195.clone.1..sunk, s32[]{:T(128)} %constant.195.clone.1..sunk) | dynamic-update-slice | bytes 1712132 | tf_op jit(solution)/shard_map/while/body/jit(dynamic_update_index_in_dim)/dynamic_update_slice | solution.py:97
  329.8 11.2 %fusion.151 = bf16[4,64,512]{2,1,0:T(8,128)(2,1)S(1)} fusion(bf16[836,4,64]{0,2,1:T(8,128)(2,1)S(1)} %bitcast.173, f32[4,836,512]{2,1,0:T(8,128)} %fusion.149, f32[4,836,512]{2,1,0:T(8,128)} %copy-done.1, f32[4,512]{1,0:T(4,128)S(1)} %log_add_fusion.2, pred[836,512]{1,0:T(8,128)(4,1)S(1)} %dynamic-slice_bitcast_fusion.2), kind=kOutput, calls=%fused_computation.10.clone.1 | convolution fusion | flops 237988672 | bytes 14823424 | tf_op jit(solution)/shard_map/while/body/eval_jaxpr/thkq,tkhe->tqhe/dot_general | solution.py:133
  341.0 12.2 %fusion.152 = f32[4,64,836]{2,1,0:T(8,128)} fusion(bf16[512,4,64]{0,2,1:T(8,128)(2,1)S(1)} %bitcast.180, f32[4,836,512]{2,1,0:T(8,128)} %fusion.149, f32[4,836,512]{2,1,0:T(8,128)} %copy-done.1, f32[4,512]{1,0:T(4,128)S(1)} %log_add_fusion.2, pred[836,512]{1,0:T(8,128)(4,1)S(1)} %dynamic-slice_bitcast_fusion.2), kind=kOutput, calls=%fused_computation.9.clone.1 | convolution fusion | flops 237988672 | bytes 15251456 | tf_op jit(solution)/shard_map/while/body/eval_jaxpr/thkq,tqhe->tkhe/dot_general | solution.py:142
  353.2 4.8 fusion.153
  362.9 19.5 %dynamic_update_slice.21 = f32[4,1,836,256]{3,0,2,1:T(4,128)} dynamic-update-slice(f32[4,1,836,256]{3,0,2,1:T(4,128)} %get-tuple-element.260, f32[1,1,836,256]{3,0,2,1:T(1,128)S(1)} %copy.84, s32[]{:T(128)S(6)} %copy.95, s32[]{:T(128)} %constant.195.clone.1..sunk, s32[]{:T(128)} %constant.195.clone.1..sunk, s32[]{:T(128)} %constant.195.clone.1..sunk) | dynamic-update-slice | bytes 1712132 | tf_op jit(solution)/shard_map/while/body/jit(dynamic_update_index_in_dim)/dynamic_update_slice | solution.py:97
  382.4 19.5 %dynamic_update_slice.22 = f32[4,1,836,256]{3,0,2,1:T(4,128)} dynamic-update-slice(f32[4,1,836,256]{3,0,2,1:T(4,128)} %get-tuple-element.261, f32[1,1,836,256]{3,0,2,1:T(1,128)S(1)} %copy.85, s32[]{:T(128)S(6)} %copy.95, s32[]{:T(128)} %constant.195.clone.1..sunk, s32[]{:T(128)} %constant.195.clone.1..sunk, s32[]{:T(128)} %constant.195.clone.1..sunk) | dynamic-update-slice | bytes 1712132 | tf_op jit(solution)/shard_map/while/body/jit(dynamic_update_index_in_dim)/dynamic_update_slice | solution.py:97
  437.1 83.3 %psum.23 = f32[256]{0:T(256)S(1)} all-reduce(f32[256]{0:T(256)} %get-tuple-element.131), channel_id=1, replica_groups=mesh['rows'=64,'dp'=4] {'rows','dp'}, use_global_device_ids=true, to_apply=%region_10.11 | all-reduce | flops 256 | bytes 2048 | tf_op jit(solution)/shard_map/psum | solution.py:231
  523.7 247.2 %all-reduce.10.cloned.1.call-done = (f32[256,768]{1,0:T(8,128)}, f32[256,256]{1,0:T(8,128)}) async-done(((f32[256,768]{1,0:T(8,128)}, f32[256,256]{1,0:T(8,128)}), (f32[256,768]{1,0:T(8,128)}, f32[256,256]{1,0:T(8,128)})) %all-reduce.10.cloned.1.call-update) | async-done | bytes 1048592 | tf_op jit(solution)/shard_map/psum | solution.py:231
  (177 shorter events, 162.2 us)
Async XLA Ops:
  7.2 19.7 %copy-start = (bf16[1,16,128,256]{3,2,1,0:T(8,128)(2,1)S(1)}, bf16[1,16,128,256]{3,2,1,0:T(8,128)(2,1)}, u32[]{:S(2)}) copy-start(bf16[1,16,128,256]{3,2,1,0:T(8,128)(2,1)} %param.19) | copy-start | bytes 3145732
  7.2 3.9 copy-start.10
  7.2 763.7 %all-reduce.10.cloned.1.call-start = ((), (), s32[]{:S(2)}) async-start(), calls=%async_computation | async-start | bytes 2097152 | tf_op jit(solution)/shard_map/psum | solution.py:231
  12.1 1.6 copy-start.2
  14.7 20.3 %collective-permute-start = (bf16[3,128,512]{2,1,0:T(8,128)(2,1)}, bf16[3,128,512]{2,1,0:T(8,128)(2,1)S(1)}, u32[]{:S(2)}, u32[]{:S(2)}) collective-permute-start(bf16[3,128,512]{2,1,0:T(8,128)(2,1)} %get-tuple-element.163), channel_id=1, source_target_pairs={{0,4},{4,8},{8,12},{12,16},{16,20},{20,24},{24,28},{28,32},{32,36}... | collective-permute-start | bytes 1179656 | tf_op jit(solution)/shard_map/ppermute | solution.py:17
  19.6 15.4 %collective-permute-start.1 = (bf16[3,128,512]{2,1,0:T(8,128)(2,1)}, bf16[3,128,512]{2,1,0:T(8,128)(2,1)}, u32[]{:S(2)}, u32[]{:S(2)}) collective-permute-start(bf16[3,128,512]{2,1,0:T(8,128)(2,1)} %get-tuple-element.164), channel_id=1, source_target_pairs={{4,0},{8,4},{12,8},{16,12},{20,16},{24,20},{28,24},{32,28},{36,32}... | collective-permute-start | bytes 1179656 | tf_op jit(solution)/shard_map/ppermute | solution.py:19
  26.9 2.6 copy-start.4
  61.4 2.9 copy-start.1
  149.2 2.9 copy-start.1
  237.1 2.9 copy-start.1
  324.9 2.9 copy-start.1
  402.0 3.6 copy-start.5
  405.5 1.2 copy-start.8
  410.4 13.9 %collective-permute-start.2 = (bf16[3,128,256]{2,1,0:T(8,128)(2,1)S(1)}, bf16[3,128,256]{2,1,0:T(8,128)(2,1)S(1)}, u32[]{:S(2)}, u32[]{:S(2)}) collective-permute-start(bf16[3,128,256]{2,1,0:T(8,128)(2,1)S(1)} %get-tuple-element.165), channel_id=1, source_target_pairs={{0,4},{4,8},{8,12},{12,16},{16,20},{20,24},{24,28},{28,32},{32,36}... | collective-permute-start | bytes 589832 | tf_op jit(solution)/shard_map/ppermute | solution.py:17
  414.1 10.2 %collective-permute-start.3 = (bf16[3,128,256]{2,1,0:T(8,128)(2,1)S(1)}, bf16[3,128,256]{2,1,0:T(8,128)(2,1)S(1)}, u32[]{:S(2)}, u32[]{:S(2)}) collective-permute-start(bf16[3,128,256]{2,1,0:T(8,128)(2,1)S(1)} %get-tuple-element.166), channel_id=1, source_target_pairs={{4,0},{8,4},{12,8},{16,12},{20,16},{24,20},{28,24},{32,28},{36,32}... | collective-permute-start | bytes 589832 | tf_op jit(solution)/shard_map/ppermute | solution.py:19
  417.0 1.2 copy-start.7
  418.3 11.0 %copy-start.9 = (bf16[16,4,32,256]{3,2,1,0:T(8,128)(2,1)}, bf16[16,4,32,256]{3,2,1,0:T(8,128)(2,1)S(1)}, u32[]{:S(2)}) copy-start(bf16[16,4,32,256]{3,2,1,0:T(8,128)(2,1)S(1)} %copy.41) | copy-start | bytes 3145732
  418.3 6.3 collective-permute-start.4
  422.0 7.0 collective-permute-start.5
  429.1 1.3 copy-start.3
  429.1 1.3 copy-start.12
  429.1 1.3 copy-start.13
  429.3 1.0 copy-start.6
  430.4 2.2 copy-start.11
Sparse Core Ops, SparseCore 0:
  520.6 250.2 all-reduce.9
where the time goes:
time: 788 us; the launch traced here: 782 us
  waiting for transfers between devices  252 us (32%)
  local copies, waits for them, and re-layouts  233 us (30%)
  matrix products  152 us (19%)
  blocking collectives  83.3 us (11%)
  other arithmetic  28.2 us (4%)
  starting transfers between devices  18 us (2%)
  between operations  14.5 us (2%)
    psum x1, waiting for transfers between devices, local(): lax.psum((grad_in_weight, grad_out_weight, grad_gain), ('rows', 'dp'))  247 us
    dynamic_update_slice x28, local copies, waits for them, and re-layouts, by_groups(): results = lax.map(step_fn, shaped)  176 us
    psum x1, blocking collectives, local(): lax.psum((grad_in_weight, grad_out_weight, grad_gain), ('rows', 'dp'))  83.3 us
    dot_general x4, matrix products, query_side(): jnp.einsum('thkq,tqhe->tkhe', grad_score, query_heads, preferred_element_...  49 us
    dot_general x4, matrix products, query_side(): jnp.einsum('thkq,tkhe->tqhe', grad_score, key_heads, preferred_element_ty...  44.8 us
    dot_general x4, matrix products, query_side(): jnp.einsum('thkq,tqhe->tkhe', weights, up_heads, preferred_element_type=j...  19.1 us
    dynamic_slice x24, local copies, waits for them, and re-layouts, by_groups(): results = lax.map(step_fn, shaped)  17.4 us
    dot_general x4, matrix products, query_side(): jnp.einsum('tqhe,tkhe->thkq', up_heads, value_heads, preferred_element_ty...  15.8 us
  transfers between devices with their start and end apart: 7, of which 2 were waited for; matrix products, arithmetic and copies ran while one was open for 2% of the time, Pallas kernels for 0%

commit v1 on v0

v1 whole, which is shorter than its diff:
```python
import math

import jax
import jax.numpy as jnp
from jax import lax
from jax.experimental import pallas as pl
from jax.experimental.pallas import tpu as pltpu
from jax.sharding import PartitionSpec as P

F32 = jnp.float32
BF16 = jnp.bfloat16
D = 256
COLS = 128
OWN = 16
FRAME = OWN + 6
PADDED = 144
NEG = -1e30
NT = (((1,), (1,)), ((), ()))
TN = (((0,), (0,)), ((), ()))


def dot(a, b, dims=(((1,), (0,)), ((), ()))):
    return lax.dot_general(a, b, dims, preferred_element_type=F32)


def attention_kernel(
    tok, up, down, cot, gain, w_in, w_out,
    gn_out, rim_up, rim_down, sums_out,
    padded, shifted, k_win, v_win, q_tiles, g_tiles, natural, attended, d_query, bias, acc, gw,
):
    here = lax.axis_index("rows")
    last = lax.axis_size("rows") - 1
    shifted[...] = jnp.zeros_like(shifted)
    gain_row = gain[...]

    def normalise(x):
        wide = x.astype(F32)
        inv = lax.rsqrt(jnp.mean(wide * wide, axis=-1, keepdims=True) + 1e-6)
        return wide * inv * gain_row

    def windows(normed, slot, frame_row):
        shifted[slot, 4 : 4 + COLS, :] = normed
        padded[frame_row] = shifted[slot].astype(BF16)
        rows = jnp.concatenate([shifted[slot, 8 * j : 8 * j + 16, :] for j in range(16)], axis=0)
        kv = dot(rows.astype(BF16), w_in[:, D:])
        k_win[frame_row] = kv[:, :D].astype(BF16).reshape(16, 16, D)
        v_win[frame_row] = kv[:, D:].astype(BF16).reshape(16, 16, D)

    def halo_row(r, carry):
        windows(normalise(up[r]), 0, r)
        windows(normalise(down[r]), 1, OWN + 3 + r)
        return carry

    def tile_order(pair):
        return [
            jnp.concatenate([pair[8 * j : 8 * j + 8], pair[COLS + 8 * j : COLS + 8 * j + 8]], axis=0)
            for j in range(16)
        ]

    def own_pair(i, carry):
        first = 2 * i
        half = i // 4
        place = pl.multiple_of((i % 4) * 16, 16)
        one = normalise(tok[first])
        two = normalise(tok[first + 1])
        windows(one, 0, first + 3)
        windows(two, 1, first + 4)
        both = jnp.concatenate([one, two], axis=0).astype(BF16)
        natural[pl.ds(first, 2)] = both.reshape(2, COLS, D)
        q = dot(both, w_in[:, :D])
        for j, tile in enumerate(tile_order(q)):
            q_tiles[half, j, pl.ds(place, 16), :] = (tile.astype(BF16).astype(F32) * 0.125).astype(BF16)
        g = dot(cot[pl.ds(first, 2)].reshape(2 * COLS, D), w_out[...], NT)
        for j, tile in enumerate(tile_order(g)):
            g_tiles[half, j, pl.ds(place, 16), :] = tile.astype(BF16)
        return carry

    lax.fori_loop(0, 3, halo_row, 0)
    lax.fori_loop(0, 8, own_pair, 0)

    key = lax.broadcasted_iota(jnp.int32, (224, D), 0)
    lane = lax.broadcasted_iota(jnp.int32, (224, D), 1)
    k_row, k_col = key // 16, key % 16
    q_row, q_col = (lane % 64) // 8, lane % 8
    near = (k_row - q_row >= 0) & (k_row - q_row <= 6) & (k_col - q_col >= 1) & (k_col - q_col <= 7)
    for half in range(2):
        if half == 0:
            inside = near & ((k_row >= 3) | (here > 0))
        else:
            inside = near & ((k_row < 11) | (here < last))
        for side in range(3):
            ok = inside
            if side == 0:
                ok = ok & (k_col >= 4)
            if side == 2:
                ok = ok & (k_col < 12)
            bias[half, side] = jnp.where(ok, 0.0, NEG)

    def zero_row(r, carry):
        acc[r] = jnp.zeros((PADDED, 2 * D), F32)
        return carry

    lax.fori_loop(0, FRAME, zero_row, 0)

    head_lane = lax.broadcasted_iota(jnp.int32, (64, D), 1) // 64

    def by_head(tile):
        return jnp.concatenate(
            [jnp.where(head_lane == h, tile, jnp.zeros_like(tile)) for h in range(4)], axis=0
        )

    def of_heads(full):
        out = full[192:256]
        for h in (2, 1, 0):
            out = jnp.where(head_lane == h, full[64 * h : 64 * h + 64], out)
        return out

    def one_tile(half, j, side):
        frame = half * 8
        k = k_win[pl.ds(frame, 14), j].reshape(224, D)
        v = v_win[pl.ds(frame, 14), j].reshape(224, D)
        q = by_head(q_tiles[half, j])
        g = by_head(g_tiles[half, j])
        s = dot(k, q, NT) + bias[half, side]
        e = jnp.exp(s - jnp.max(s, axis=0, keepdims=True))
        p = e * (1.0 / jnp.sum(e, axis=0, keepdims=True))
        weights = p.astype(BF16)
        dp = dot(v, g, NT)
        delta = jnp.sum(p * dp, axis=0, keepdims=True)
        ds = (p * (dp - delta)).astype(BF16)
        place = pl.ds(pl.multiple_of(8 * j, 8), 16)
        acc[pl.ds(frame, 14), place, :D] += dot(ds, q).reshape(14, 16, D)
        acc[pl.ds(frame, 14), place, D:] += dot(weights, g).reshape(14, 16, D)
        att = of_heads(dot(weights, v, TN))
        dq = of_heads(dot(ds, k, TN)) * 0.125
        return att.reshape(8, 8, D), dq.reshape(8, 8, D)

    def tile_pair(i, carry):
        half, jp = i // 8, i % 8
        a0, d0 = one_tile(half, 2 * jp, jnp.where(jp == 0, 0, 1))
        a1, d1 = one_tile(half, 2 * jp + 1, jnp.where(jp == 7, 2, 1))
        rows = pl.ds(half * 8, 8)
        cols = pl.ds(pl.multiple_of(16 * jp, 16), 16)
        attended[rows, cols, :] = jnp.concatenate([a0, a1], axis=1).astype(BF16)
        d_query[rows, cols, :] = jnp.concatenate([d0, d1], axis=1).astype(BF16)
        return carry

    lax.fori_loop(0, 16, tile_pair, 0)

    gw[...] = jnp.zeros_like(gw)

    def key_row(r, carry):
        both = acc[r].astype(BF16)
        gw[:, D : 3 * D] += dot(padded[r], both, TN)
        acc[r, :, :D] = dot(both, w_in[:, D:], NT)
        return carry

    lax.fori_loop(0, FRAME, key_row, 0)
    rim_up[...] = acc[0:3, 4 : 4 + COLS, :D].astype(BF16)
    rim_down[...] = acc[OWN + 3 : FRAME, 4 : 4 + COLS, :D].astype(BF16)

    def query_rows(i, carry):
        rows = pl.ds(2 * i, 2)
        dq = d_query[rows].reshape(2 * COLS, D)
        gn = dot(dq, w_in[:, :D], NT).reshape(2, COLS, D)
        gn_out[rows] = gn + acc[pl.ds(2 * i + 3, 2), 4 : 4 + COLS, :D]
        gw[:, :D] += dot(natural[rows].reshape(2 * COLS, D), dq, TN)
        gw[:, 3 * D :] += dot(
            attended[rows].reshape(2 * COLS, D), cot[rows].reshape(2 * COLS, D), TN
        )
        return carry

    lax.fori_loop(0, 8, query_rows, 0)
    for g in range(16):
        for h in range(2):
            sums_out[2 * g + h] = gw[16 * g : 16 * g + 16, 512 * h : 512 * h + 512].astype(BF16)


def attention(tok, up, down, cot, gain, w_in, w_out):
    vmem = pl.BlockSpec(memory_space=pltpu.VMEM)
    return pl.pallas_call(
        attention_kernel,
        out_shape=(
            jax.ShapeDtypeStruct((OWN, COLS, D), F32),
            jax.ShapeDtypeStruct((3, COLS, D), BF16),
            jax.ShapeDtypeStruct((3, COLS, D), BF16),
            jax.ShapeDtypeStruct((32, 16, 512), BF16),
        ),
        in_specs=[vmem] * 7,
        out_specs=(vmem,) * 4,
        scratch_shapes=[
            pltpu.VMEM((FRAME, PADDED, D), BF16),
            pltpu.VMEM((2, PADDED, D), F32),
            pltpu.VMEM((FRAME, 16, 16, D), BF16),
            pltpu.VMEM((FRAME, 16, 16, D), BF16),
            pltpu.VMEM((2, 16, 64, D), BF16),
            pltpu.VMEM((2, 16, 64, D), BF16),
            pltpu.VMEM((OWN, COLS, D), BF16),
            pltpu.VMEM((OWN, COLS, D), BF16),
            pltpu.VMEM((OWN, COLS, D), BF16),
            pltpu.VMEM((2, 3, 224, D), F32),
            pltpu.VMEM((FRAME, PADDED, 2 * D), F32),
            pltpu.VMEM((D, 4 * D), F32),
        ],
        compiler_params=pltpu.CompilerParams(vmem_limit_bytes=56 * 1024 * 1024),
        cost_estimate=pl.CostEstimate(flops=16_000_000_000, bytes_accessed=6_000_000, transcendentals=2_000_000),
    )(tok, up, down, cot, gain, w_in, w_out)


def sum_kernel(
    factor, mine, w_in, gain, g_in, g_out, g_gain,
    plane_got, z_parts, z_got, z_full, full,
    plane_send, plane_recv, z_send, z_recv, back_send, back_recv, out_send, out_recv,
):
    rows = lax.axis_index("rows")
    x = lax.axis_index("dp")
    core = rows % 2
    z = (rows // 2) % 8
    y = rows // 16
    me = (y * 4 + x) * 2 + core

    def in_plane(i):
        to_y, to_x, to_core = (y + i // 8) % 4, (x + (i // 2) % 4) % 4, (core + i % 2) % 2
        where = {"rows": (to_y * 8 + z) * 2 + to_core, "dp": to_x}
        return where, (to_y * 4 + to_x) * 2 + to_core

    def along_z(i):
        to_z = (z + i) % 8
        return {"rows": (y * 8 + to_z) * 2 + core, "dp": x}, to_z

    def remote(src, dst, send, recv, where):
        return pltpu.make_async_remote_copy(
            src_ref=src, dst_ref=dst, send_sem=send, recv_sem=recv,
            device_id=where, device_id_type=pl.DeviceIdType.MESH,
        )

    barrier = pltpu.get_barrier_semaphore()

    def greet_plane(i, carry):
        pl.semaphore_signal(barrier, inc=1, device_id=in_plane(i)[0], device_id_type=pl.DeviceIdType.MESH)
        return carry

    def greet_z(i, carry):
        pl.semaphore_signal(barrier, inc=1, device_id=along_z(i)[0], device_id_type=pl.DeviceIdType.MESH)
        return carry

    lax.fori_loop(1, 32, greet_plane, 0)
    lax.fori_loop(1, 8, greet_z, 0)
    pl.semaphore_wait(barrier, 38)

    def scatter(i):
        where, index = in_plane(i)
        return remote(mine.at[index], plane_got.at[i], plane_send.at[i], plane_recv.at[i], where)

    def z_scatter(i):
        where, index = along_z(i)
        return remote(z_parts.at[index], z_got.at[i], z_send.at[i], z_recv.at[i], where)

    def z_gather(i):
        where, index = along_z(i)
        return remote(z_full.at[z], z_full.at[z], back_send.at[i], back_recv.at[i], where)

    def gather(i):
        where, index = in_plane(i)
        return remote(full.at[me], full.at[me], out_send.at[i], out_recv.at[i], where)

    def start(make):
        def body(i, carry):
            make(i).start()
            return carry
        return body

    def wait_send(make):
        def body(i, carry):
            make(i).wait_send()
            return carry
        return body

    def wait_recv(make):
        def body(i, carry):
            make(i).wait_recv()
            return carry
        return body

    lax.fori_loop(1, 32, start(scatter), 0)

    def add_plane(i, total):
        scatter(i).wait_recv()
        return total + plane_got[i].astype(F32)

    total = lax.fori_loop(1, 32, add_plane, mine[me].astype(F32))
    for p in range(8):
        r, c = 8 * (p // 4), 128 * (p % 4)
        z_parts[p] = total[r : r + 8, c : c + 128]
    lax.fori_loop(1, 8, start(z_scatter), 0)

    def add_z(i, piece):
        z_scatter(i).wait_recv()
        return piece + z_got[i]

    z_full[z] = lax.fori_loop(1, 8, add_z, z_parts[z])
    lax.fori_loop(1, 8, start(z_gather), 0)
    lax.fori_loop(1, 8, wait_recv(z_gather), 0)
    done = jnp.concatenate(
        [jnp.concatenate([z_full[4 * a + c] for c in range(4)], axis=1) for a in range(2)], axis=0
    )
    full[me] = done.astype(BF16)
    lax.fori_loop(1, 32, start(gather), 0)
    lax.fori_loop(1, 32, wait_recv(gather), 0)
    for g in range(16):
        span = slice(16 * g, 16 * g + 16)
        left = full[2 * g].astype(F32) * factor
        right = full[2 * g + 1].astype(F32) * factor
        g_in[span, :512] = left
        g_in[span, 512:] = right[:, :256]
        g_out[span, :] = right[:, 256:]
    per_row = jnp.sum(g_in[...] * w_in[...].astype(F32), axis=1, keepdims=True)
    g_gain[...] = jnp.transpose(jnp.broadcast_to(per_row, (D, 128)))[0:1] / gain[...]
    lax.fori_loop(1, 32, wait_send(scatter), 0)
    lax.fori_loop(1, 8, wait_send(z_scatter), 0)
    lax.fori_loop(1, 8, wait_send(z_gather), 0)
    lax.fori_loop(1, 32, wait_send(gather), 0)


def sum_all(mine, w_in, gain, factor):
    vmem = pl.BlockSpec(memory_space=pltpu.VMEM)
    dma = pltpu.SemaphoreType.DMA
    return pl.pallas_call(
        lambda *refs: sum_kernel(factor, *refs),
        out_shape=(
            jax.ShapeDtypeStruct((D, 3 * D), F32),
            jax.ShapeDtypeStruct((D, D), F32),
            jax.ShapeDtypeStruct((1, D), F32),
        ),
        in_specs=[vmem] * 3,
        out_specs=(vmem,) * 3,
        scratch_shapes=[
            pltpu.VMEM((32, 16, 512), BF16),
            pltpu.VMEM((8, 8, 128), F32),
            pltpu.VMEM((8, 8, 128), F32),
            pltpu.VMEM((8, 8, 128), F32),
            pltpu.VMEM((32, 16, 512), BF16),
            dma((32,)), dma((32,)), dma((8,)), dma((8,)),
            dma((8,)), dma((8,)), dma((32,)), dma((32,)),
        ],
        compiler_params=pltpu.CompilerParams(
            collective_id=0, has_side_effects=True, vmem_limit_bytes=32 * 1024 * 1024
        ),
    )(mine, w_in, gain)


def halo(first, final):
    count = lax.axis_size("rows")
    from_left = lax.ppermute(final, "rows", [(i, i + 1) for i in range(count - 1)])
    from_right = lax.ppermute(first, "rows", [(i + 1, i) for i in range(count - 1)])
    return from_left, from_right


def local(tokens, norm_gain, in_weight, out_weight, cotangent):
    tok = tokens[0]
    gain = norm_gain.reshape(1, D)
    up, down = halo(tok[:3], tok[-3:])
    gn, rim_up, rim_down, mine = attention(tok, up, down, cotangent[0], gain, in_weight, out_weight)
    add_top, add_bottom = halo(rim_up, rim_down)
    factor = 1.0 / math.sqrt(lax.axis_size("rows") * lax.axis_size("dp") * OWN * COLS)
    g_in, g_out, g_gain = sum_all(mine, in_weight, gain, factor)
    wide = tok.astype(F32)
    inv = lax.rsqrt(jnp.mean(wide * wide, axis=-1, keepdims=True) + 1e-6)
    gn = gn.at[:3].add(add_top.astype(F32)).at[-3:].add(add_bottom.astype(F32))
    gained = gn * norm_gain
    grad_tokens = inv * (gained - wide * inv * inv * jnp.mean(gained * wide, axis=-1, keepdims=True))
    return grad_tokens.astype(BF16)[None], g_in, g_out, g_gain.reshape(D)


def solution(mesh):
    return jax.shard_map(
        local,
        mesh=mesh,
        in_specs=(P("dp", "rows", None, None), P(), P(), P(), P("dp", "rows", None, None)),
        out_specs=(P("dp", "rows", None, None), P(), P(), P()),
        check_vma=False,
    )
```

time: 788 us -> 108 us (0.14)
  waiting for transfers between devices: 252 us -> 2.6 us
  local copies, waits for them, and re-layouts: 233 us -> 4.92 us
  matrix products: 152 us -> 0 us
  blocking collectives: 83.3 us -> 0 us
  Pallas kernels: 0 us -> 78.1 us
  other arithmetic: 28.2 us -> 7.49 us
  between operations: 14.5 us -> 0.73 us
    psum x1 -> x0, waiting for transfers between devices: 247 us -> none  [local(): lax.psum((grad_in_weight, grad_out_weight, grad_gain), ('rows', 'dp'))]
    dynamic_update_slice x28 -> x0, local copies, waits for them, and re-layouts: 176 us -> none  [by_groups(): results = lax.map(step_fn, shaped)]
    dot_general x29 -> x0, matrix products: 152 us -> none  [the longest x4 49 us: query_side(): jnp.einsum('thkq,tqhe->tkhe', grad_score, query_heads, preferred_element_...]
    psum x1 -> x0, blocking collectives: 83.3 us -> none  [local(): lax.psum((grad_in_weight, grad_out_weight, grad_gain), ('rows', 'dp'))]
    pallas_call x0 -> x2, Pallas kernels: none -> 78.1 us  [the longest x1 42.6 us: sum_all(): pl.pallas_call(lambda *refs: sum_kernel(factor, *refs), out_shape=(jax.Sh...]
    dynamic_slice x24 -> x0, local copies, waits for them, and re-layouts: 17.4 us -> none  [by_groups(): results = lax.map(step_fn, shaped)]
    while x10 -> x0, local copies, waits for them, and re-layouts: 12.9 us -> none  [the longest x2 7.35 us: by_groups(): results = lax.map(step_fn, shaped)]
    slice x13 -> x1, local copies, waits for them, and re-layouts: 11.7 us -> 1.05 us  [local(): up, down = halo(tok[:3], tok[-3:])]
  transfers between devices with their start and end apart: 7 -> 4, of which waited for: 2 -> 2; matrix products, arithmetic and copies ran while one was open for 2% -> 2% of each run, Pallas kernels for 0% -> 40%
where the time goes in v1:
time: 108 us; the launch traced here: 107 us
  Pallas kernels  78.1 us (72%)
  starting transfers between devices  13.4 us (12%)
  other arithmetic  7.49 us (7%)
  local copies, waits for them, and re-layouts  4.92 us (5%)
  waiting for transfers between devices  2.6 us (2%)
    pallas_call x1, Pallas kernels, sum_all(): pl.pallas_call(lambda *refs: sum_kernel(factor, *refs), out_shape=(jax.Sh...  42.6 us
    pallas_call x1, Pallas kernels, attention(): pl.pallas_call(attention_kernel, out_shape=(jax.ShapeDtypeStruct((OWN, CO...  35.5 us
    ppermute x2, starting transfers between devices, halo(): lax.ppermute(first, 'rows', [(i + 1, i) for i in range(count - 1)])  7.07 us
    ppermute x2, starting transfers between devices, halo(): lax.ppermute(final, 'rows', [(i, i + 1) for i in range(count - 1)])  6.29 us
    unnamed x17, local copies, waits for them, and re-layouts  3.87 us
    scatter-add x2, other arithmetic, local(): gn = gn.at[:3].add(add_top.astype(F32)).at[-3:].add(add_bottom.astype(F32))  3.6 us
    reduce_sum x1, other arithmetic, local(): inv = lax.rsqrt(jnp.mean(wide * wide, axis=-1, keepdims=True) + 1e-06)  2.36 us
  transfers between devices with their start and end apart: 4, of which 2 were waited for; matrix products, arithmetic and copies ran while one was open for 2% of the time, Pallas kernels for 40%

profile of v1, /device:TPU:1, one launch (start us, length us, event | category | flops | bytes accessed | tf_op | source)
XLA Modules:
  0.0 107.2 jit_solution(12156167155742226146)
XLA Ops:
  0.6 1.1 slice_bitcast_fusion
  1.7 5.1 %collective-permute-start.1 = (bf16[3,128,256]{2,1,0:T(8,128)(2,1)S(1)}, bf16[3,128,256]{2,1,0:T(8,128)(2,1)S(1)}, u32[]{:S(2)}, u32[]{:S(2)}) collective-permute-start(bf16[3,128,256]{2,1,0:T(8,128)(2,1)S(1)} %get-tuple-element.44), channel_id=1, source_target_pairs={{4,0},{8,4},{12,8},{16,12},{20,16},{24,20},{28,24},{32,28},{36,32}... | collective-permute-start | bytes 589832 | tf_op jit(solution)/shard_map/ppermute | solution.py:355
  6.8 1.9 %collective-permute-start = (bf16[3,128,256]{2,1,0:T(8,128)(2,1)S(1)}, bf16[3,128,256]{2,1,0:T(8,128)(2,1)S(1)}, u32[]{:S(2)}, u32[]{:S(2)}) collective-permute-start(bf16[3,128,256]{2,1,0:T(8,128)(2,1)S(1)} %get-tuple-element.45), channel_id=1, source_target_pairs={{0,4},{4,8},{8,12},{12,16},{16,20},{20,24},{24,28},{28,32},{32,36}... | collective-permute-start | bytes 589832 | tf_op jit(solution)/shard_map/ppermute | solution.py:354
  8.8 1.2 %collective-permute-done.1.down = bf16[3,128,256]{2,1,0:T(8,128)(2,1)S(1)} collective-permute-done((bf16[3,128,256]{2,1,0:T(8,128)(2,1)S(1)}, bf16[3,128,256]{2,1,0:T(8,128)(2,1)S(1)}, u32[]{:S(2)}, u32[]{:S(2)}) %collective-permute-start.1) | collective-permute-done | bytes 196640 | tf_op jit(solution)/shard_map/ppermute | solution.py:355
  10.0 1.4 %collective-permute-done.up = bf16[3,128,256]{2,1,0:T(8,128)(2,1)S(1)} collective-permute-done((bf16[3,128,256]{2,1,0:T(8,128)(2,1)S(1)}, bf16[3,128,256]{2,1,0:T(8,128)(2,1)S(1)}, u32[]{:S(2)}, u32[]{:S(2)}) %collective-permute-start) | collective-permute-done | bytes 196640 | tf_op jit(solution)/shard_map/ppermute | solution.py:354
  11.4 0.0 copy-done.5
  11.4 0.7 copy-done.6
  12.0 35.5 %shard_map.84 = (f32[16,128,256]{2,1,0:T(8,128)}, bf16[3,128,256]{2,1,0:T(8,128)(2,1)}, bf16[3,128,256]{2,1,0:T(8,128)(2,1)}, bf16[32,16,512]{2,1,0:T(8,128)(2,1)}) custom-call(bf16[16,128,256]{2,1,0:T(8,128)(2,1)} %bitcast.16, bf16[3,128,256]{2,1,0:T(8,128)(2,1)} %copy-done.6, bf16[3,128,256]{2,1,0:T(8,128)(2,1)} %copy-done.5, ...), custom_call_target="tpu_custom_call" | custom-call | flops 16000000000 | bytes 6000000 | tf_op jit(solution)/shard_map/pallas_call | solution.py:181
  47.6 4.4 %collective-permute-start.2 = (bf16[3,128,256]{2,1,0:T(8,128)(2,1)}, bf16[3,128,256]{2,1,0:T(8,128)(2,1)S(1)}, u32[]{:S(2)}, u32[]{:S(2)}) collective-permute-start(bf16[3,128,256]{2,1,0:T(8,128)(2,1)} %get-tuple-element.36), channel_id=1, source_target_pairs={{0,4},{4,8},{8,12},{12,16},{16,20},{20,24},{24,28},{28,32},{32,36}... | collective-permute-start | bytes 589832 | tf_op jit(solution)/shard_map/ppermute | solution.py:354
  51.9 1.9 %collective-permute-start.3 = (bf16[3,128,256]{2,1,0:T(8,128)(2,1)}, bf16[3,128,256]{2,1,0:T(8,128)(2,1)S(1)}, u32[]{:S(2)}, u32[]{:S(2)}) collective-permute-start(bf16[3,128,256]{2,1,0:T(8,128)(2,1)} %get-tuple-element.37), channel_id=1, source_target_pairs={{4,0},{8,4},{12,8},{16,12},{20,16},{24,20},{28,24},{32,28},{36,32}... | collective-permute-start | bytes 589832 | tf_op jit(solution)/shard_map/ppermute | solution.py:355
  53.9 0.0 copy-done.1
  53.9 0.0 copy-done.2
  53.9 0.0 copy-start
  53.9 1.0 copy-done
  54.9 42.6 %shard_map.85 = (f32[256,768]{1,0:T(8,128)S(1)}, f32[256,256]{1,0:T(8,128)S(1)}, f32[1,256]{1,0:T(1,128)S(1)}) custom-call(bf16[32,16,512]{2,1,0:T(8,128)(2,1)S(1)} %copy-done, bf16[256,768]{1,0:T(8,128)(2,1)S(1)} %copy-done.1, f32[1,256]{1,0:T(1,128)S(1)} %bitcast.14), custom_call_target="tpu_custom_call" | custom-call | tf_op jit(solution)/shard_map/pallas_call | solution.py:328
  97.5 0.0 collective-permute-done.2
  97.5 1.8 %add_dynamic-update-slice_fusion = f32[16,128,256]{2,1,0:T(8,128)} fusion(f32[16,128,256]{2,1,0:T(8,128)} %get-tuple-element.35, bf16[3,128,256]{2,1,0:T(8,128)(2,1)S(1)} %collective-permute-done.2), kind=kLoop, calls=%fused_computation.13 | loop fusion | flops 196608 | bytes 983040 | tf_op jit(solution)/shard_map/scatter-add | solution.py:369
  99.3 0.0 collective-permute-done.3
  99.3 1.8 %fusion.8 = f32[16,128,256]{2,1,0:T(8,128)} fusion(f32[16,128,256]{2,1,0:T(8,128)} %add_dynamic-update-slice_fusion, bf16[3,128,256]{2,1,0:T(8,128)(2,1)S(1)} %collective-permute-done.3), kind=kLoop, calls=%fused_computation.12 | loop fusion | flops 196608 | bytes 983040 | tf_op jit(solution)/shard_map/scatter-add | solution.py:369
  101.1 2.4 %fusion = (f32[16,128]{1,0:T(8,128)S(1)}, f32[16,128]{1,0:T(8,128)S(1)}) fusion(bf16[1,16,128,256]{3,2,1,0:T(8,128)(2,1)S(1)} %copy-done.4, f32[16,128,256]{2,1,0:T(8,128)} %fusion.8, f32[256]{0:T(256)S(1)} %copy-done.2), kind=kLoop, calls=%fused_computation.3 | loop fusion | flops 3141632 | bytes 3163136 | tf_op jit(solution)/shard_map/reduce_sum | solution.py:368
  103.5 1.5 %fusion.7 = bf16[1,16,128,256]{3,2,1,0:T(8,128)(2,1)} fusion(f32[16,128,256]{2,1,0:T(8,128)S(1)} %copy-done.3, f32[16,128]{1,0:T(8,128)S(1)} %get-tuple-element.47, f32[256]{0:T(256)S(1)} %copy-done.2, f32[16,128]{1,0:T(8,128)S(1)} %get-tuple-element.46, bf16[1,16,128,256]{3,2,1,0:T(8,128)(2,1)S(1)} %copy-done.4), kind=kLoop, calls=%fused_computation.10 | loop fusion | flops 4194304 | bytes 4211712 | tf_op jit(solution)/shard_map/broadcast_in_dim | solution.py:372
  105.1 0.9 copy.14
  105.9 0.7 copy.15
  106.6 0.6 copy.16
  (9 shorter events, 0.0 us)
Async XLA Ops:
  1.7 8.3 %collective-permute-start.1 = (bf16[3,128,256]{2,1,0:T(8,128)(2,1)S(1)}, bf16[3,128,256]{2,1,0:T(8,128)(2,1)S(1)}, u32[]{:S(2)}, u32[]{:S(2)}) collective-permute-start(bf16[3,128,256]{2,1,0:T(8,128)(2,1)S(1)} %get-tuple-element.44), channel_id=1, source_target_pairs={{4,0},{8,4},{12,8},{16,12},{20,16},{24,20},{28,24},{32,28},{36,32}... | collective-permute-start | bytes 589832 | tf_op jit(solution)/shard_map/ppermute | solution.py:355
  6.8 4.5 %collective-permute-start = (bf16[3,128,256]{2,1,0:T(8,128)(2,1)S(1)}, bf16[3,128,256]{2,1,0:T(8,128)(2,1)S(1)}, u32[]{:S(2)}, u32[]{:S(2)}) collective-permute-start(bf16[3,128,256]{2,1,0:T(8,128)(2,1)S(1)} %get-tuple-element.45), channel_id=1, source_target_pairs={{0,4},{4,8},{8,12},{12,16},{16,20},{20,24},{24,28},{28,32},{32,36}... | collective-permute-start | bytes 589832 | tf_op jit(solution)/shard_map/ppermute | solution.py:354
  10.0 1.4 %copy-start.5 = (bf16[3,128,256]{2,1,0:T(8,128)(2,1)}, bf16[3,128,256]{2,1,0:T(8,128)(2,1)S(1)}, u32[]{:S(2)}) copy-start(bf16[3,128,256]{2,1,0:T(8,128)(2,1)S(1)} %collective-permute-done.1.down) | copy-start | bytes 589828
  11.4 0.7 copy-start.6
  12.0 41.8 %copy-start.1 = (bf16[256,768]{1,0:T(8,128)(2,1)S(1)}, bf16[256,768]{1,0:T(8,128)(2,1)}, u32[]{:S(2)}) copy-start(bf16[256,768]{1,0:T(8,128)(2,1)} %refs_1_.1) | copy-start | bytes 1179652
  12.0 41.8 %copy-start.2 = (f32[256]{0:T(256)S(1)}, f32[256]{0:T(256)}, u32[]{:S(2)}) copy-start(f32[256]{0:T(256)} %param.10) | copy-start | bytes 3076
  12.0 89.1 %copy-start.4 = (bf16[1,16,128,256]{3,2,1,0:T(8,128)(2,1)S(1)}, bf16[1,16,128,256]{3,2,1,0:T(8,128)(2,1)}, u32[]{:S(2)}) copy-start(bf16[1,16,128,256]{3,2,1,0:T(8,128)(2,1)} %param.9) | copy-start | bytes 3145732
  47.6 50.0 %collective-permute-start.2 = (bf16[3,128,256]{2,1,0:T(8,128)(2,1)}, bf16[3,128,256]{2,1,0:T(8,128)(2,1)S(1)}, u32[]{:S(2)}, u32[]{:S(2)}) collective-permute-start(bf16[3,128,256]{2,1,0:T(8,128)(2,1)} %get-tuple-element.36), channel_id=1, source_target_pairs={{0,4},{4,8},{8,12},{12,16},{16,20},{20,24},{24,28},{28,32},{32,36}... | collective-permute-start | bytes 589832 | tf_op jit(solution)/shard_map/ppermute | solution.py:354
  51.9 47.4 %collective-permute-start.3 = (bf16[3,128,256]{2,1,0:T(8,128)(2,1)}, bf16[3,128,256]{2,1,0:T(8,128)(2,1)S(1)}, u32[]{:S(2)}, u32[]{:S(2)}) collective-permute-start(bf16[3,128,256]{2,1,0:T(8,128)(2,1)} %get-tuple-element.37), channel_id=1, source_target_pairs={{4,0},{8,4},{12,8},{16,12},{20,16},{24,20},{28,24},{32,28},{36,32}... | collective-permute-start | bytes 589832 | tf_op jit(solution)/shard_map/ppermute | solution.py:355
  53.9 1.0 copy-start
  101.1 2.4 %copy-start.3 = (f32[16,128,256]{2,1,0:T(8,128)S(1)}, f32[16,128,256]{2,1,0:T(8,128)}, u32[]{:S(2)}) copy-start(f32[16,128,256]{2,1,0:T(8,128)} %fusion.8) | copy-start | bytes 6291460

commit v2 on v1

v2 whole, which is shorter than its diff:
```python
import math
from types import SimpleNamespace

import jax
import jax.numpy as jnp
from jax import lax
from jax.experimental import pallas as pl
from jax.experimental.pallas import tpu as pltpu
from jax.sharding import PartitionSpec as P

F32 = jnp.float32
BF16 = jnp.bfloat16
D = 256
COLS = 128
OWN = 16
FRAME = OWN + 6
PADDED = 144
NEG = -1e30
NT = (((1,), (1,)), ((), ()))
TN = (((0,), (0,)), ((), ()))
VMEM_BYTES = 58 * 1024 * 1024

BUFFERS = {
    "halo": ((2, 3, COLS, D), BF16),
    "shifted": ((2, PADDED, D), F32),
    "normed": ((FRAME, COLS, D), BF16),
    "k_win": ((FRAME, 16, 16, D), BF16),
    "v_win": ((FRAME, 16, 16, D), BF16),
    "q_tiles": ((2, 16, 64, D), BF16),
    "g_tiles": ((2, 16, 64, D), BF16),
    "attended": ((OWN, COLS, D), BF16),
    "joined": ((FRAME, COLS, 3 * D), BF16),
    "bias": ((2, 3, 224, D), F32),
    "acc": ((FRAME, PADDED, 2 * D), F32),
    "gn": ((OWN, COLS, D), F32),
    "sums": ((32, 16, 512), BF16),
    "rim_out": ((2, 3, COLS, D), BF16),
    "rim_in": ((2, 3, COLS, D), BF16),
}


def dot(a, b, dims=(((1,), (0,)), ((), ()))):
    return lax.dot_general(a, b, dims, preferred_element_type=F32)


def inverse_rms(wide):
    return lax.rsqrt(jnp.mean(wide * wide, axis=-1, keepdims=True) + 1e-6)


def windows(b, x, slot, frame_row):
    wide = x.astype(F32)
    normed = wide * inverse_rms(wide) * b.gain[...]
    b.normed[frame_row] = normed.astype(BF16)
    b.shifted[slot, 4 : 4 + COLS, :] = normed
    rows = jnp.concatenate([b.shifted[slot, 8 * j : 8 * j + 16, :] for j in range(16)], axis=0)
    kv = dot(rows.astype(BF16), b.w_in[:, D:])
    b.k_win[frame_row] = kv[:, :D].astype(BF16).reshape(16, 16, D)
    b.v_win[frame_row] = kv[:, D:].astype(BF16).reshape(16, 16, D)


def clear(b):
    b.shifted[...] = jnp.zeros_like(b.shifted)
    for r in range(3):
        b.joined[r, :, :D] = jnp.zeros((COLS, D), BF16)
        b.joined[OWN + 3 + r, :, :D] = jnp.zeros((COLS, D), BF16)

    def zero_row(r, carry):
        b.acc[r] = jnp.zeros((PADDED, 2 * D), F32)
        return carry

    lax.fori_loop(0, FRAME, zero_row, 0)


def mask(b, here, last):
    key = lax.broadcasted_iota(jnp.int32, (224, D), 0)
    lane = lax.broadcasted_iota(jnp.int32, (224, D), 1)
    k_row, k_col = key // 16, key % 16
    q_row, q_col = (lane % 64) // 8, lane % 8
    near = (k_row - q_row >= 0) & (k_row - q_row <= 6) & (k_col - q_col >= 1) & (k_col - q_col <= 7)
    for half in range(2):
        if half == 0:
            inside = near & ((k_row >= 3) | (here > 0))
        else:
            inside = near & ((k_row < 11) | (here < last))
        for side in range(3):
            ok = inside
            if side == 0:
                ok = ok & (k_col >= 4)
            if side == 2:
                ok = ok & (k_col < 12)
            b.bias[half, side] = jnp.where(ok, 0.0, NEG)


def own_rows(b):
    def tile_order(pair):
        return [
            jnp.concatenate([pair[8 * j : 8 * j + 8], pair[COLS + 8 * j : COLS + 8 * j + 8]], axis=0)
            for j in range(16)
        ]

    def own_pair(i, carry):
        first = 2 * i
        half = i // 4
        place = pl.multiple_of((i % 4) * 16, 16)
        windows(b, b.tok[first], 0, first + 3)
        windows(b, b.tok[first + 1], 1, first + 4)
        both = b.normed[pl.ds(first + 3, 2)].reshape(2 * COLS, D)
        q = dot(both, b.w_in[:, :D])
        for j, tile in enumerate(tile_order(q)):
            b.q_tiles[half, j, pl.ds(place, 16), :] = (tile.astype(BF16).astype(F32) * 0.125).astype(BF16)
        g = dot(b.cot[pl.ds(first, 2)].reshape(2 * COLS, D), b.w_out[...], NT)
        for j, tile in enumerate(tile_order(g)):
            b.g_tiles[half, j, pl.ds(place, 16), :] = tile.astype(BF16)
        return carry

    lax.fori_loop(0, 8, own_pair, 0)


def halo_rows(b):
    def halo_row(r, carry):
        windows(b, b.halo[0, r], 0, r)
        windows(b, b.halo[1, r], 1, OWN + 3 + r)
        return carry

    lax.fori_loop(0, 3, halo_row, 0)


def attend(b):
    head_lane = lax.broadcasted_iota(jnp.int32, (64, D), 1) // 64

    def by_head(tile):
        return jnp.concatenate(
            [jnp.where(head_lane == h, tile, jnp.zeros_like(tile)) for h in range(4)], axis=0
        )

    def of_heads(full):
        out = full[192:256]
        for h in (2, 1, 0):
            out = jnp.where(head_lane == h, full[64 * h : 64 * h + 64], out)
        return out

    def one_tile(half, j, side):
        frame = half * 8
        k = b.k_win[pl.ds(frame, 14), j].reshape(224, D)
        v = b.v_win[pl.ds(frame, 14), j].reshape(224, D)
        q = by_head(b.q_tiles[half, j])
        g = by_head(b.g_tiles[half, j])
        s = dot(k, q, NT) + b.bias[half, side]
        e = jnp.exp(s - jnp.max(s, axis=0, keepdims=True))
        p = e * (1.0 / jnp.sum(e, axis=0, keepdims=True))
        weights = p.astype(BF16)
        dp = dot(v, g, NT)
        delta = jnp.sum(p * dp, axis=0, keepdims=True)
        ds = (p * (dp - delta)).astype(BF16)
        place = pl.ds(pl.multiple_of(8 * j, 8), 16)
        b.acc[pl.ds(frame, 14), place, :D] += dot(ds, q).reshape(14, 16, D)
        b.acc[pl.ds(frame, 14), place, D:] += dot(weights, g).reshape(14, 16, D)
        att = of_heads(dot(weights, v, TN))
        dq = of_heads(dot(ds, k, TN)) * 0.125
        return att.reshape(8, 8, D), dq.reshape(8, 8, D)

    def tile_pair(i, carry):
        half, jp = i // 8, i % 8
        a0, d0 = one_tile(half, 2 * jp, jnp.where(jp == 0, 0, 1))
        a1, d1 = one_tile(half, 2 * jp + 1, jnp.where(jp == 7, 2, 1))
        cols = pl.ds(pl.multiple_of(16 * jp, 16), 16)
        b.attended[pl.ds(half * 8, 8), cols, :] = jnp.concatenate([a0, a1], axis=1).astype(BF16)
        b.joined[pl.ds(half * 8 + 3, 8), cols, :D] = jnp.concatenate([d0, d1], axis=1).astype(BF16)
        return carry

    lax.fori_loop(0, 16, tile_pair, 0)


def weight_sums(b):
    def key_row(r, carry):
        b.joined[r, :, D:] = b.acc[r, 4 : 4 + COLS, :].astype(BF16)
        return carry

    lax.fori_loop(0, FRAME, key_row, 0)
    g_in = dot(b.normed[...].reshape(FRAME * COLS, D), b.joined[...].reshape(FRAME * COLS, 3 * D), TN)
    g_out = dot(b.attended[...].reshape(OWN * COLS, D), b.cot[...].reshape(OWN * COLS, D), TN)
    for g in range(16):
        span = slice(16 * g, 16 * g + 16)
        b.sums[2 * g] = g_in[span, :512].astype(BF16)
        b.sums[2 * g + 1] = jnp.concatenate([g_in[span, 512:], g_out[span]], axis=1).astype(BF16)


def rim_rows(b):
    for side, first in ((0, 0), (1, OWN + 3)):
        rows = b.joined[first : first + 3].reshape(3 * COLS, 3 * D)
        b.rim_out[side] = dot(rows, b.w_in[...], NT).reshape(3, COLS, D).astype(BF16)


def own_gn(b):
    def four(i, carry):
        rows = b.joined[pl.ds(3 + 4 * i, 4)].reshape(4 * COLS, 3 * D)
        b.gn[pl.ds(4 * i, 4)] = dot(rows, b.w_in[...], NT).reshape(4, COLS, D)
        return carry

    lax.fori_loop(0, 4, four, 0)


def finish(b, row, rim=None):
    wide = b.tok[row].astype(F32)
    inv = inverse_rms(wide)
    gn = b.gn[row]
    if rim is not None:
        gn = gn + rim.astype(F32)
    gained = gn * b.gain[...]
    mean = jnp.mean(gained * wide, axis=-1, keepdims=True)
    b.gt[row] = (inv * (gained - wide * (inv * inv * mean))).astype(BF16)


def finish_rows(b, low, high):
    def body(r, carry):
        finish(b, r)
        return carry

    lax.fori_loop(low, high, body, 0)


def block_kernel(factor, names, *refs):
    b = SimpleNamespace(**dict(zip(names, refs)))
    rows = lax.axis_index("rows")
    count = lax.axis_size("rows")
    x = lax.axis_index("dp")
    core = rows % 2
    z = (rows // 2) % 8
    y = rows // 16
    me = (y * 4 + x) * 2 + core
    before = {"rows": (rows + count - 1) % count, "dp": x}
    after = {"rows": (rows + 1) % count, "dp": x}

    def in_plane(i):
        to_y, to_x, to_core = (y + i // 8) % 4, (x + (i // 2) % 4) % 4, (core + i % 2) % 2
        where = {"rows": (to_y * 8 + z) * 2 + to_core, "dp": to_x}
        return where, (to_y * 4 + to_x) * 2 + to_core

    def along_z(i):
        to_z = (z + i) % 8
        return {"rows": (y * 8 + to_z) * 2 + core, "dp": x}, to_z

    def remote(src, dst, send, recv, where):
        return pltpu.make_async_remote_copy(
            src_ref=src, dst_ref=dst, send_sem=send, recv_sem=recv,
            device_id=where, device_id_type=pl.DeviceIdType.MESH,
        )

    barrier = pltpu.get_barrier_semaphore()

    def greet(where):
        pl.semaphore_signal(barrier, inc=1, device_id=where, device_id_type=pl.DeviceIdType.MESH)

    def greet_plane(i, carry):
        greet(in_plane(i)[0])
        return carry

    def greet_z(i, carry):
        greet(along_z(i)[0])
        return carry

    greet(before)
    greet(after)
    lax.fori_loop(1, 32, greet_plane, 0)
    lax.fori_loop(1, 8, greet_z, 0)
    clear(b)
    pl.semaphore_wait(barrier, 40)

    def halo_copies():
        return (
            remote(b.tok.at[pl.ds(OWN - 3, 3)], b.halo.at[0], b.near_send.at[0], b.near_recv.at[0], after),
            remote(b.tok.at[pl.ds(0, 3)], b.halo.at[1], b.near_send.at[1], b.near_recv.at[1], before),
        )

    def rim_copies():
        return (
            remote(b.rim_out.at[0], b.rim_in.at[1], b.near_send.at[2], b.near_recv.at[2], before),
            remote(b.rim_out.at[1], b.rim_in.at[0], b.near_send.at[3], b.near_recv.at[3], after),
        )

    def scatter(i):
        where, index = in_plane(i)
        return remote(b.sums.at[index], b.plane_got.at[i], b.plane_send.at[i], b.plane_recv.at[i], where)

    def z_scatter(i):
        where, index = along_z(i)
        return remote(b.z_parts.at[index], b.z_got.at[i], b.z_send.at[i], b.z_recv.at[i], where)

    def z_gather(i):
        where, index = along_z(i)
        return remote(b.z_full.at[z], b.z_full.at[z], b.back_send.at[i], b.back_recv.at[i], where)

    def gather(i):
        where, index = in_plane(i)
        return remote(b.full.at[me], b.full.at[me], b.out_send.at[i], b.out_recv.at[i], where)

    def each(make, high, act):
        def body(i, carry):
            act(make(i))
            return carry

        lax.fori_loop(1, high, body, 0)

    def start(copy):
        copy.start()

    def wait_send(copy):
        copy.wait_send()

    def wait_recv(copy):
        copy.wait_recv()

    for copy in halo_copies():
        copy.start()
    mask(b, rows, count - 1)
    own_rows(b)
    for copy in halo_copies():
        copy.wait_recv()
    halo_rows(b)
    attend(b)
    weight_sums(b)
    each(scatter, 32, start)
    rim_rows(b)
    for copy in rim_copies():
        copy.start()
    own_gn(b)

    def add_plane(i, total):
        scatter(i).wait_recv()
        return total + b.plane_got[i].astype(F32)

    total = lax.fori_loop(1, 32, add_plane, b.sums[me].astype(F32))
    for p in range(8):
        r, c = 8 * (p // 4), 128 * (p % 4)
        b.z_parts[p] = total[r : r + 8, c : c + 128]
    each(z_scatter, 8, start)
    finish_rows(b, 3, 8)

    def add_z(i, piece):
        z_scatter(i).wait_recv()
        return piece + b.z_got[i]

    b.z_full[z] = lax.fori_loop(1, 8, add_z, b.z_parts[z])
    each(z_gather, 8, start)
    finish_rows(b, 8, 13)
    each(z_gather, 8, wait_recv)
    done = jnp.concatenate(
        [jnp.concatenate([b.z_full[4 * a + c] for c in range(4)], axis=1) for a in range(2)], axis=0
    )
    b.full[me] = done.astype(BF16)
    each(gather, 32, start)
    for copy in rim_copies():
        copy.wait_recv()

    def edge(r, carry):
        finish(b, r, b.rim_in[0, r])
        finish(b, OWN - 3 + r, b.rim_in[1, r])
        return carry

    lax.fori_loop(0, 3, edge, 0)
    each(gather, 32, wait_recv)
    for g in range(16):
        span = slice(16 * g, 16 * g + 16)
        left = b.full[2 * g].astype(F32) * factor
        right = b.full[2 * g + 1].astype(F32) * factor
        b.g_in[span, :512] = left
        b.g_in[span, 512:] = right[:, :256]
        b.g_out[span, :] = right[:, 256:]
    per_row = jnp.sum(b.g_in[...] * b.w_in[...].astype(F32), axis=1, keepdims=True)
    b.g_gain[...] = jnp.transpose(jnp.broadcast_to(per_row, (D, 128)))[0:1] / b.gain[...]
    for copy in halo_copies() + rim_copies():
        copy.wait_send()
    each(scatter, 32, wait_send)
    each(z_scatter, 8, wait_send)
    each(z_gather, 8, wait_send)
    each(gather, 32, wait_send)


def block(tok, cot, gain, w_in, w_out, factor):
    vmem = pl.BlockSpec(memory_space=pltpu.VMEM)
    dma = pltpu.SemaphoreType.DMA
    outs = {
        "gt": ((OWN, COLS, D), BF16),
        "g_in": ((D, 3 * D), F32),
        "g_out": ((D, D), F32),
        "g_gain": ((1, D), F32),
    }
    slots = {
        "plane_got": ((32, 16, 512), BF16),
        "z_parts": ((8, 8, 128), F32),
        "z_got": ((8, 8, 128), F32),
        "z_full": ((8, 8, 128), F32),
        "full": ((32, 16, 512), BF16),
    }
    sems = {
        "near_send": 4, "near_recv": 4, "plane_send": 32, "plane_recv": 32, "z_send": 8, "z_recv": 8,
        "back_send": 8, "back_recv": 8, "out_send": 32, "out_recv": 32,
    }
    names = ["tok", "cot", "gain", "w_in", "w_out", *outs, *BUFFERS, *slots, *sems]

    def kernel(*refs):
        block_kernel(factor, names, *refs)

    return pl.pallas_call(
        kernel,
        out_shape=tuple(jax.ShapeDtypeStruct(*o) for o in outs.values()),
        in_specs=[vmem] * 5,
        out_specs=(vmem,) * 4,
        scratch_shapes=[
            *(pltpu.VMEM(*s) for s in BUFFERS.values()),
            *(pltpu.VMEM(*s) for s in slots.values()),
            *(dma((n,)) for n in sems.values()),
        ],
        compiler_params=pltpu.CompilerParams(
            collective_id=0, has_side_effects=True, vmem_limit_bytes=VMEM_BYTES
        ),
    )(tok, cot, gain, w_in, w_out)


def local(tokens, norm_gain, in_weight, out_weight, cotangent):
    factor = 1.0 / math.sqrt(lax.axis_size("rows") * lax.axis_size("dp") * OWN * COLS)
    gt, g_in, g_out, g_gain = block(
        tokens[0], cotangent[0], norm_gain.reshape(1, D), in_weight, out_weight, factor
    )
    return gt[None], g_in, g_out, g_gain.reshape(D)


def solution(mesh):
    return jax.shard_map(
        local,
        mesh=mesh,
        in_specs=(P("dp", "rows", None, None), P(), P(), P(), P("dp", "rows", None, None)),
        out_specs=(P("dp", "rows", None, None), P(), P(), P()),
        check_vma=False,
    )
```

time: 108 us -> 73.5 us (0.68)
  starting transfers between devices: 13.4 us -> 0 us
  Pallas kernels: 78.1 us -> 67.9 us
  other arithmetic: 7.49 us -> 0 us
  waiting for transfers between devices: 2.6 us -> 0 us
    ppermute x4 -> x0, starting transfers between devices: 13.4 us -> none  [the longest x2 7.07 us: halo(): lax.ppermute(first, 'rows', [(i + 1, i) for i in range(count - 1)])]
    pallas_call x2 -> x1, Pallas kernels: 78.1 us -> 67.9 us  [block(): pl.pallas_call(kernel, out_shape=tuple((jax.ShapeDtypeStruct(*o) for o in...]
    scatter-add x2 -> x0, other arithmetic: 3.6 us -> none  [local(): gn = gn.at[:3].add(add_top.astype(F32)).at[-3:].add(add_bottom.astype(F32))]
    ppermute x4 -> x0, waiting for transfers between devices: 2.6 us -> none  [the longest x2 1.4 us: halo(): lax.ppermute(final, 'rows', [(i, i + 1) for i in range(count - 1)])]
    reduce_sum x1 -> x0, other arithmetic: 2.36 us -> none  [local(): inv = lax.rsqrt(jnp.mean(wide * wide, axis=-1, keepdims=True) + 1e-06)]
    broadcast_in_dim x1 -> x0, other arithmetic: 1.53 us -> none  [local(): return (grad_tokens.astype(BF16)[None], g_in, g_out, g_gain.reshape(D))]
    unnamed x17 -> x10, local copies, waits for them, and re-layouts: 3.87 us -> 4.72 us
  transfers between devices with their start and end apart: 4 -> 0, of which waited for: 2 -> 0; matrix products, arithmetic and copies ran while one was open for 2% -> 0% of each run, Pallas kernels for 40% -> 0%
where the time goes in v2:
time: 73.5 us; the launch traced here: 73.3 us
  Pallas kernels  67.9 us (92%)
  local copies, waits for them, and re-layouts  4.72 us (6%)
    pallas_call x1, Pallas kernels, block(): pl.pallas_call(kernel, out_shape=tuple((jax.ShapeDtypeStruct(*o) for o in...  67.9 us
    unnamed x10, local copies, waits for them, and re-layouts  4.72 us

profile of v2, /device:TPU:1, one launch (start us, length us, event | category | flops | bytes accessed | tf_op | source)
XLA Modules:
  0.0 73.3 jit_solution(18222477565662760587)
XLA Ops:
  0.6 67.9 %shard_map.84 = (bf16[16,128,256]{2,1,0:T(8,128)(2,1)}, f32[256,768]{1,0:T(8,128)}, f32[256,256]{1,0:T(8,128)}, f32[1,256]{1,0:T(1,128)}) custom-call(bf16[16,128,256]{2,1,0:T(8,128)(2,1)} %bitcast.5, bf16[16,128,256]{2,1,0:T(8,128)(2,1)} %bitcast.6, f32[1,256]{1,0:T(1,128)} %bitcast.8, bf16[256,768]{1,0:T(8,128)(2,1)} %refs_3_.1, bf16[256,256]{1,0:T(8,128)(2,1)} %refs_4_.1), custom_call_target="tpu_custom_call" | custom-call | tf_op jit(solution)/shard_map/pallas_call | solution.py:404
  68.6 0.0 copy-start
  68.6 2.4 %copy.13 = bf16[1,16,128,256]{3,2,1,0:T(8,128)(2,1)} copy(bf16[1,16,128,256]{3,2,1,0:T(8,128)(2,1)} %bitcast.7) | data formatting | bytes 2097152
  70.9 0.0 copy-done
  70.9 0.0 copy-start.1
  70.9 0.9 %copy.14 = f32[256,768]{1,0:T(8,128)} copy(f32[256,768]{1,0:T(8,128)S(1)} %copy-done) | data formatting | bytes 1572864
  71.8 0.2 copy-done.1
  72.0 0.0 copy-start.2
  72.0 0.7 copy.15
  72.7 0.0 copy-done.2
  72.7 0.6 copy.16
Async XLA Ops:
  68.6 2.4 %copy-start = (f32[256,768]{1,0:T(8,128)S(1)}, f32[256,768]{1,0:T(8,128)}, u32[]{:S(2)}) copy-start(f32[256,768]{1,0:T(8,128)} %get-tuple-element.17) | copy-start | bytes 2359300
  70.9 1.1 %copy-start.1 = (f32[256,256]{1,0:T(8,128)S(1)}, f32[256,256]{1,0:T(8,128)}, u32[]{:S(2)}) copy-start(f32[256,256]{1,0:T(8,128)} %get-tuple-element.18) | copy-start | bytes 786436
  72.0 0.7 copy-start.2

commit v3 on v2

--- a/solution.py
+++ b/solution.py
@@ -160,15 +160,18 @@
         return att.reshape(8, 8, D), dq.reshape(8, 8, D)
 
     def tile_pair(i, carry):
-        half, jp = i // 8, i % 8
+        one_pair(0, i)
+        one_pair(1, i)
+        return carry
+
+    def one_pair(half, jp):
         a0, d0 = one_tile(half, 2 * jp, jnp.where(jp == 0, 0, 1))
         a1, d1 = one_tile(half, 2 * jp + 1, jnp.where(jp == 7, 2, 1))
         cols = pl.ds(pl.multiple_of(16 * jp, 16), 16)
         b.attended[pl.ds(half * 8, 8), cols, :] = jnp.concatenate([a0, a1], axis=1).astype(BF16)
         b.joined[pl.ds(half * 8 + 3, 8), cols, :D] = jnp.concatenate([d0, d1], axis=1).astype(BF16)
-        return carry
-
-    lax.fori_loop(0, 16, tile_pair, 0)
+
+    lax.fori_loop(0, 8, tile_pair, 0)
 
 
 def weight_sums(b):
@@ -219,7 +222,7 @@
     lax.fori_loop(low, high, body, 0)
 
 
-def block_kernel(factor, names, *refs):
+def block_kernel(names, *refs):
     b = SimpleNamespace(**dict(zip(names, refs)))
     rows = lax.axis_index("rows")
     count = lax.axis_size("rows")
@@ -227,18 +230,22 @@
     core = rows % 2
     z = (rows // 2) % 8
     y = rows // 16
-    me = (y * 4 + x) * 2 + core
+    me = y * 4 + x
     before = {"rows": (rows + count - 1) % count, "dp": x}
     after = {"rows": (rows + 1) % count, "dp": x}
+    partner = {"rows": rows + 1 - 2 * core, "dp": x}
+    mine = 16 * core
+    other = 16 - mine
 
     def in_plane(i):
-        to_y, to_x, to_core = (y + i // 8) % 4, (x + (i // 2) % 4) % 4, (core + i % 2) % 2
-        where = {"rows": (to_y * 8 + z) * 2 + to_core, "dp": to_x}
-        return where, (to_y * 4 + to_x) * 2 + to_core
+        to_y, to_x = (y + i // 4) % 4, (x + i % 4) % 4
+        return {"rows": (to_y * 8 + z) * 2 + core, "dp": to_x}, to_y * 4 + to_x
+
+    def from_plane(i):
+        return ((y + 4 - i // 4) % 4) * 4 + (x + 4 - i % 4) % 4
 
     def along_z(i):
-        to_z = (z + i) % 8
-        return {"rows": (y * 8 + to_z) * 2 + core, "dp": x}, to_z
+        return {"rows": (y * 8 + (z + i) % 8) * 2 + core, "dp": x}
 
     def remote(src, dst, send, recv, where):
         return pltpu.make_async_remote_copy(
@@ -256,15 +263,16 @@
         return carry
 
     def greet_z(i, carry):
-        greet(along_z(i)[0])
+        greet(along_z(i))
         return carry
 
     greet(before)
     greet(after)
-    lax.fori_loop(1, 32, greet_plane, 0)
+    greet(partner)
+    lax.fori_loop(1, 16, greet_plane, 0)
     lax.fori_loop(1, 8, greet_z, 0)
     clear(b)
-    pl.semaphore_wait(barrier, 40)
+    pl.semaphore_wait(barrier, 25)
 
     def halo_copies():
         return (
@@ -278,28 +286,32 @@
             remote(b.rim_out.at[1], b.rim_in.at[0], b.near_send.at[3], b.near_recv.at[3], after),
         )
 
+    def core_scatter(i):
+        place = in_plane(i)[1]
+        return remote(b.sums.at[other + place], b.core_got.at[i], b.core_send.at[i], b.core_recv.at[i], partner)
+
     def scatter(i):
-        where, index = in_plane(i)
-        return remote(b.sums.at[index], b.plane_got.at[i], b.plane_send.at[i], b.plane_recv.at[i], where)
-
-    def z_scatter(i):
-        where, index = along_z(i)
-        return remote(b.z_parts.at[index], b.z_got.at[i], b.z_send.at[i], b.z_recv.at[i], where)
-
-    def z_gather(i):
-        where, index = along_z(i)
-        return remote(b.z_full.at[z], b.z_full.at[z], b.back_send.at[i], b.back_recv.at[i], where)
+        where, place = in_plane(i)
+        return remote(b.paired.at[i], b.plane_got.at[i], b.plane_send.at[i], b.plane_recv.at[i], where)
+
+    def z_share(i):
+        where = along_z(i)
+        return remote(b.z_all.at[z], b.z_all.at[z], b.z_send.at[i], b.z_recv.at[i], where)
 
     def gather(i):
-        where, index = in_plane(i)
-        return remote(b.full.at[me], b.full.at[me], b.out_send.at[i], b.out_recv.at[i], where)
-
-    def each(make, high, act):
+        where, place = in_plane(i)
+        return remote(b.full.at[mine + me], b.full.at[mine + me], b.out_send.at[i], b.out_recv.at[i], where)
+
+    def core_gather(i):
+        chunk = b.full.at[mine + from_plane(i)]
+        return remote(chunk, chunk, b.last_send.at[i], b.last_recv.at[i], partner)
+
+    def each(make, low, high, act):
         def body(i, carry):
             act(make(i))
             return carry
 
-        lax.fori_loop(1, high, body, 0)
+        lax.fori_loop(low, high, body, 0)
 
     def start(copy):
         copy.start()
@@ -319,36 +331,39 @@
     halo_rows(b)
     attend(b)
     weight_sums(b)
-    each(scatter, 32, start)
+    each(core_scatter, 1, 16, start)
+    core_scatter(0).start()
     rim_rows(b)
     for copy in rim_copies():
         copy.start()
+
+    def pair(i):
+        core_scatter(i).wait_recv()
+        return b.sums[mine + in_plane(i)[1]].astype(F32) + b.core_got[i].astype(F32)
+
+    def pair_and_send(i, carry):
+        b.paired[i] = pair(i).astype(BF16)
+        scatter(i).start()
+        return carry
+
+    lax.fori_loop(1, 16, pair_and_send, 0)
     own_gn(b)
 
     def add_plane(i, total):
         scatter(i).wait_recv()
         return total + b.plane_got[i].astype(F32)
 
-    total = lax.fori_loop(1, 32, add_plane, b.sums[me].astype(F32))
-    for p in range(8):
-        r, c = 8 * (p // 4), 128 * (p % 4)
-        b.z_parts[p] = total[r : r + 8, c : c + 128]
-    each(z_scatter, 8, start)
-    finish_rows(b, 3, 8)
-
-    def add_z(i, piece):
-        z_scatter(i).wait_recv()
-        return piece + b.z_got[i]
-
-    b.z_full[z] = lax.fori_loop(1, 8, add_z, b.z_parts[z])
-    each(z_gather, 8, start)
-    finish_rows(b, 8, 13)
-    each(z_gather, 8, wait_recv)
-    done = jnp.concatenate(
-        [jnp.concatenate([b.z_full[4 * a + c] for c in range(4)], axis=1) for a in range(2)], axis=0
-    )
-    b.full[me] = done.astype(BF16)
-    each(gather, 32, start)
+    total = lax.fori_loop(1, 16, add_plane, pair(0))
+    b.z_all[z] = total.astype(BF16)
+    each(z_share, 1, 8, start)
+    finish_rows(b, 3, 13)
+    each(z_share, 1, 8, wait_recv)
+    whole = b.z_all[0].astype(F32)
+    for i in range(1, 8):
+        whole = whole + b.z_all[i].astype(F32)
+    b.full[mine + me] = whole.astype(BF16)
+    each(gather, 1, 16, start)
+    core_gather(0).start()
     for copy in rim_copies():
         copy.wait_recv()
 
@@ -358,54 +373,48 @@
         return carry
 
     lax.fori_loop(0, 3, edge, 0)
-    each(gather, 32, wait_recv)
-    for g in range(16):
-        span = slice(16 * g, 16 * g + 16)
-        left = b.full[2 * g].astype(F32) * factor
-        right = b.full[2 * g + 1].astype(F32) * factor
-        b.g_in[span, :512] = left
-        b.g_in[span, 512:] = right[:, :256]
-        b.g_out[span, :] = right[:, 256:]
-    per_row = jnp.sum(b.g_in[...] * b.w_in[...].astype(F32), axis=1, keepdims=True)
-    b.g_gain[...] = jnp.transpose(jnp.broadcast_to(per_row, (D, 128)))[0:1] / b.gain[...]
+
+    def pass_on(i, carry):
+        gather(i).wait_recv()
+        core_gather(i).start()
+        return carry
+
+    lax.fori_loop(1, 16, pass_on, 0)
+    each(core_gather, 0, 16, wait_recv)
     for copy in halo_copies() + rim_copies():
         copy.wait_send()
-    each(scatter, 32, wait_send)
-    each(z_scatter, 8, wait_send)
-    each(z_gather, 8, wait_send)
-    each(gather, 32, wait_send)
-
-
-def block(tok, cot, gain, w_in, w_out, factor):
+    each(core_scatter, 0, 16, wait_send)
+    each(scatter, 1, 16, wait_send)
+    each(z_share, 1, 8, wait_send)
+    each(gather, 1, 16, wait_send)
+    each(core_gather, 0, 16, wait_send)
+
+
+def block(tok, cot, gain, w_in, w_out):
     vmem = pl.BlockSpec(memory_space=pltpu.VMEM)
     dma = pltpu.SemaphoreType.DMA
-    outs = {
-        "gt": ((OWN, COLS, D), BF16),
-        "g_in": ((D, 3 * D), F32),
-        "g_out": ((D, D), F32),
-        "g_gain": ((1, D), F32),
-    }
+    outs = {"gt": ((OWN, COLS, D), BF16), "full": ((32, 16, 512), BF16)}
     slots = {
-        "plane_got": ((32, 16, 512), BF16),
-        "z_parts": ((8, 8, 128), F32),
-        "z_got": ((8, 8, 128), F32),
-        "z_full": ((8, 8, 128), F32),
-        "full": ((32, 16, 512), BF16),
+        "core_got": ((16, 16, 512), BF16),
+        "paired": ((16, 16, 512), BF16),
+        "plane_got": ((16, 16, 512), BF16),
+        "z_all": ((8, 16, 512), BF16),
     }
     sems = {
-        "near_send": 4, "near_recv": 4, "plane_send": 32, "plane_recv": 32, "z_send": 8, "z_recv": 8,
-        "back_send": 8, "back_recv": 8, "out_send": 32, "out_recv": 32,
+        "near_send": 4, "near_recv": 4, "core_send": 16, "core_recv": 16, "plane_send": 16, "plane_recv": 16,
+        "z_send": 8, "z_recv": 8, "out_send": 16, "out_recv": 16,
+        "last_send": 16, "last_recv": 16,
     }
     names = ["tok", "cot", "gain", "w_in", "w_out", *outs, *BUFFERS, *slots, *sems]
 
     def kernel(*refs):
-        block_kernel(factor, names, *refs)
+        block_kernel(names, *refs)
 
     return pl.pallas_call(
         kernel,
         out_shape=tuple(jax.ShapeDtypeStruct(*o) for o in outs.values()),
         in_specs=[vmem] * 5,
-        out_specs=(vmem,) * 4,
+        out_specs=(vmem,) * 2,
         scratch_shapes=[
             *(pltpu.VMEM(*s) for s in BUFFERS.values()),
             *(pltpu.VMEM(*s) for s in slots.values()),
@@ -417,11 +426,50 @@
     )(tok, cot, gain, w_in, w_out)
 
 
+def outputs(gt, full, gain, w_in, factor):
+    def kernel(gt_ref, full_hbm, gain_ref, w_ref, gt_out, g_in, g_out, g_gain, full_ref, sem):
+        copy = pltpu.make_async_copy(gt_ref, gt_out, sem.at[0])
+        copy.start()
+        fetch = pltpu.make_async_copy(full_hbm, full_ref, sem.at[1])
+        fetch.start()
+        fetch.wait()
+        per_row = []
+        for g in range(16):
+            span = slice(16 * g, 16 * g + 16)
+            left = full_ref[2 * g].astype(F32) * factor
+            right = full_ref[2 * g + 1].astype(F32) * factor
+            g_in[span, :512] = left
+            g_in[span, 512:] = right[:, :256]
+            g_out[span, :] = right[:, 256:]
+            w = w_ref[span, :].astype(F32)
+            term = jnp.sum(left * w[:, :512], axis=1, keepdims=True)
+            per_row.append(term + jnp.sum(right[:, :256] * w[:, 512:], axis=1, keepdims=True))
+        column = jnp.broadcast_to(jnp.concatenate(per_row, axis=0), (D, 128))
+        g_gain[...] = jnp.transpose(column)[0:1] / gain_ref[...]
+        copy.wait()
+
+    vmem = pl.BlockSpec(memory_space=pltpu.VMEM)
+    hbm = pl.BlockSpec(memory_space=pltpu.HBM)
+    return pl.pallas_call(
+        kernel,
+        out_shape=(
+            jax.ShapeDtypeStruct((OWN, COLS, D), BF16),
+            jax.ShapeDtypeStruct((D, 3 * D), F32),
+            jax.ShapeDtypeStruct((D, D), F32),
+            jax.ShapeDtypeStruct((1, D), F32),
+        ),
+        in_specs=[hbm, hbm, vmem, vmem],
+        out_specs=(hbm, vmem, vmem, vmem),
+        scratch_shapes=[pltpu.VMEM((32, 16, 512), BF16), pltpu.SemaphoreType.DMA((2,))],
+        compiler_params=pltpu.CompilerParams(vmem_limit_bytes=VMEM_BYTES),
+    )(gt, full, gain, w_in)
+
+
 def local(tokens, norm_gain, in_weight, out_weight, cotangent):
     factor = 1.0 / math.sqrt(lax.axis_size("rows") * lax.axis_size("dp") * OWN * COLS)
-    gt, g_in, g_out, g_gain = block(
-        tokens[0], cotangent[0], norm_gain.reshape(1, D), in_weight, out_weight, factor
-    )
+    gain = norm_gain.reshape(1, D)
+    gt, full = block(tokens[0], cotangent[0], gain, in_weight, out_weight)
+    gt, g_in, g_out, g_gain = outputs(gt, full, gain, in_weight, factor)
     return gt[None], g_in, g_out, g_gain.reshape(D)
 
 

time: 73.5 us -> 94.6 us (1.29)
  Pallas kernels: 67.9 us -> 93.8 us
  local copies, waits for them, and re-layouts: 4.72 us -> 0 us
    pallas_call x0 -> x1, Pallas kernels: none -> 34.9 us  [outputs(): pl.pallas_call(kernel, out_shape=(jax.ShapeDtypeStruct((OWN, COLS, D), BF...]
    pallas_call x1, Pallas kernels: 67.9 us -> 58.9 us  [block(): pl.pallas_call(kernel, out_shape=tuple((jax.ShapeDtypeStruct(*o) for o in...]
    unnamed x10 -> x0, local copies, waits for them, and re-layouts: 4.72 us -> none
where the time goes in v3:
time: 94.6 us; the launch traced here: 94.4 us
  Pallas kernels  93.8 us (99%)
    pallas_call x1, Pallas kernels, block(): pl.pallas_call(kernel, out_shape=tuple((jax.ShapeDtypeStruct(*o) for o in...  58.9 us
    pallas_call x1, Pallas kernels, outputs(): pl.pallas_call(kernel, out_shape=(jax.ShapeDtypeStruct((OWN, COLS, D), BF...  34.9 us

profile of v3, /device:TPU:1, one launch (start us, length us, event | category | flops | bytes accessed | tf_op | source)
XLA Modules:
  0.0 94.4 jit_solution(13496686828811306650)
XLA Ops:
  0.6 58.9 %shard_map.84 = (bf16[16,128,256]{2,1,0:T(8,128)(2,1)}, bf16[32,16,512]{2,1,0:T(8,128)(2,1)}) custom-call(bf16[16,128,256]{2,1,0:T(8,128)(2,1)} %bitcast.5, bf16[16,128,256]{2,1,0:T(8,128)(2,1)} %bitcast.6, f32[1,256]{1,0:T(1,128)} %bitcast.7, bf16[256,768]{1,0:T(8,128)(2,1)} %w_ref.1, bf16[256,256]{1,0:T(8,128)(2,1)} %refs_4_.1), custom_call_target="tpu_custom_call" | custom-call | tf_op jit(solution)/shard_map/pallas_call | solution.py:413
  59.6 34.9 %shard_map.85 = (bf16[16,128,256]{2,1,0:T(8,128)(2,1)}, f32[256,768]{1,0:T(8,128)}, f32[256,256]{1,0:T(8,128)}, f32[1,256]{1,0:T(1,128)}) custom-call(bf16[16,128,256]{2,1,0:T(8,128)(2,1)} %get-tuple-element.10.gt_ref, bf16[32,16,512]{2,1,0:T(8,128)(2,1)} %get-tuple-element.11.full_hbm, f32[1,256]{1,0:T(1,128)} %bitcast.8, bf16[256,768]{1,0:T(8,128)(2,1)} %w_ref.1), custom_call_target="tpu_custom_call" | custom-call | tf_op jit(solution)/shard_map/pallas_call | solution.py:453

commit v4 on v3

--- a/solution.py
+++ b/solution.py
@@ -427,28 +427,43 @@
 
 
 def outputs(gt, full, gain, w_in, factor):
-    def kernel(gt_ref, full_hbm, gain_ref, w_ref, gt_out, g_in, g_out, g_gain, full_ref, sem):
-        copy = pltpu.make_async_copy(gt_ref, gt_out, sem.at[0])
-        copy.start()
-        fetch = pltpu.make_async_copy(full_hbm, full_ref, sem.at[1])
-        fetch.start()
-        fetch.wait()
-        per_row = []
-        for g in range(16):
-            span = slice(16 * g, 16 * g + 16)
-            left = full_ref[2 * g].astype(F32) * factor
-            right = full_ref[2 * g + 1].astype(F32) * factor
-            g_in[span, :512] = left
-            g_in[span, 512:] = right[:, :256]
-            g_out[span, :] = right[:, 256:]
-            w = w_ref[span, :].astype(F32)
-            term = jnp.sum(left * w[:, :512], axis=1, keepdims=True)
-            per_row.append(term + jnp.sum(right[:, :256] * w[:, 512:], axis=1, keepdims=True))
-        column = jnp.broadcast_to(jnp.concatenate(per_row, axis=0), (D, 128))
-        g_gain[...] = jnp.transpose(column)[0:1] / gain_ref[...]
-        copy.wait()
-
-    vmem = pl.BlockSpec(memory_space=pltpu.VMEM)
+    def kernel(gt_hbm, full_hbm, gain_hbm, w_hbm, gt_out, g_in_out, g_out_out, g_gain_out,
+               rows, full_ref, gain_ref, w, g_in, g_out, g_gain, sem):
+        quarters = [pl.ds(4 * i, 4) for i in range(4)]
+        spans = [pl.ds(64 * i, 64) for i in range(4)]
+
+        def copies(first, pairs):
+            return [pltpu.make_async_copy(src, dst, sem.at[first + i]) for i, (src, dst) in enumerate(pairs)]
+
+        parts = copies(0, [(full_hbm.at[pl.ds(8 * i, 8)], full_ref.at[pl.ds(8 * i, 8)]) for i in range(4)])
+        small = copies(4, [(w_hbm, w), (gain_hbm, gain_ref)])
+        reads = copies(6, [(gt_hbm.at[r], rows.at[r]) for r in quarters])
+        writes = copies(10, [(rows.at[r], gt_out.at[r]) for r in quarters])
+        in_writes = copies(14, [(g_in.at[r], g_in_out.at[r]) for r in spans])
+        out_writes = copies(18, [(g_out.at[r], g_out_out.at[r]) for r in spans])
+        gain_write = pltpu.make_async_copy(g_gain, g_gain_out, sem.at[22])
+        for copy in parts + small + reads:
+            copy.start()
+        for i in range(4):
+            parts[i].wait()
+            for g in range(4 * i, 4 * i + 4):
+                span = slice(16 * g, 16 * g + 16)
+                right = full_ref[2 * g + 1].astype(F32) * factor
+                g_in[span, :512] = full_ref[2 * g].astype(F32) * factor
+                g_in[span, 512:] = right[:, :256]
+                g_out[span, :] = right[:, 256:]
+            in_writes[i].start()
+            out_writes[i].start()
+            reads[i].wait()
+            writes[i].start()
+        for copy in small:
+            copy.wait()
+        per_row = jnp.sum(g_in[...] * w[...].astype(F32), axis=1, keepdims=True)
+        g_gain[...] = jnp.transpose(jnp.broadcast_to(per_row, (D, 128)))[0:1] / gain_ref[...]
+        gain_write.start()
+        for copy in writes + in_writes + out_writes + [gain_write]:
+            copy.wait()
+
     hbm = pl.BlockSpec(memory_space=pltpu.HBM)
     return pl.pallas_call(
         kernel,
@@ -458,9 +473,18 @@
             jax.ShapeDtypeStruct((D, D), F32),
             jax.ShapeDtypeStruct((1, D), F32),
         ),
-        in_specs=[hbm, hbm, vmem, vmem],
-        out_specs=(hbm, vmem, vmem, vmem),
-        scratch_shapes=[pltpu.VMEM((32, 16, 512), BF16), pltpu.SemaphoreType.DMA((2,))],
+        in_specs=[hbm] * 4,
+        out_specs=(hbm,) * 4,
+        scratch_shapes=[
+            pltpu.VMEM((OWN, COLS, D), BF16),
+            pltpu.VMEM((32, 16, 512), BF16),
+            pltpu.VMEM((1, D), F32),
+            pltpu.VMEM((D, 3 * D), BF16),
+            pltpu.VMEM((D, 3 * D), F32),
+            pltpu.VMEM((D, D), F32),
+            pltpu.VMEM((1, D), F32),
+            pltpu.SemaphoreType.DMA((23,)),
+        ],
         compiler_params=pltpu.CompilerParams(vmem_limit_bytes=VMEM_BYTES),
     )(gt, full, gain, w_in)
 

time: 94.6 us -> 62.5 us (0.66)
  Pallas kernels: 93.8 us -> 61.7 us
    pallas_call x1, Pallas kernels: 34.9 us -> 2.78 us  [outputs(): pl.pallas_call(kernel, out_shape=(jax.ShapeDtypeStruct((OWN, COLS, D), BF...]
where the time goes in v4:
time: 62.5 us; the launch traced here: 62.3 us
  Pallas kernels  61.7 us (99%)
  between operations  0.64 us (1%)
    pallas_call x1, Pallas kernels, block(): pl.pallas_call(kernel, out_shape=tuple((jax.ShapeDtypeStruct(*o) for o in...  58.9 us
    pallas_call x1, Pallas kernels, outputs(): pl.pallas_call(kernel, out_shape=(jax.ShapeDtypeStruct((OWN, COLS, D), BF...  2.78 us

profile of v4, /device:TPU:1, one launch (start us, length us, event | category | flops | bytes accessed | tf_op | source)
XLA Modules:
  0.0 62.3 jit_solution(10362454824849526422)
XLA Ops:
  0.6 58.9 %shard_map.84 = (bf16[16,128,256]{2,1,0:T(8,128)(2,1)}, bf16[32,16,512]{2,1,0:T(8,128)(2,1)}) custom-call(bf16[16,128,256]{2,1,0:T(8,128)(2,1)} %bitcast.5, bf16[16,128,256]{2,1,0:T(8,128)(2,1)} %bitcast.6, f32[1,256]{1,0:T(1,128)} %bitcast.7, bf16[256,768]{1,0:T(8,128)(2,1)} %w_hbm.1, bf16[256,256]{1,0:T(8,128)(2,1)} %refs_4_.1), custom_call_target="tpu_custom_call" | custom-call | tf_op jit(solution)/shard_map/pallas_call | solution.py:413
  59.6 2.8 %shard_map.85 = (bf16[16,128,256]{2,1,0:T(8,128)(2,1)}, f32[256,768]{1,0:T(8,128)}, f32[256,256]{1,0:T(8,128)}, f32[1,256]{1,0:T(1,128)}) custom-call(bf16[16,128,256]{2,1,0:T(8,128)(2,1)} %get-tuple-element.10.gt_hbm, bf16[32,16,512]{2,1,0:T(8,128)(2,1)} %get-tuple-element.11.full_hbm, f32[1,256]{1,0:T(1,128)} %bitcast.8, bf16[256,768]{1,0:T(8,128)(2,1)} %w_hbm.1), custom_call_target="tpu_custom_call" | custom-call | tf_op jit(solution)/shard_map/pallas_call | solution.py:468

commit v5 on v4

--- a/solution.py
+++ b/solution.py
@@ -139,39 +139,40 @@
             out = jnp.where(head_lane == h, full[64 * h : 64 * h + 64], out)
         return out
 
-    def one_tile(half, j, side):
-        frame = half * 8
-        k = b.k_win[pl.ds(frame, 14), j].reshape(224, D)
-        v = b.v_win[pl.ds(frame, 14), j].reshape(224, D)
-        q = by_head(b.q_tiles[half, j])
-        g = by_head(b.g_tiles[half, j])
-        s = dot(k, q, NT) + b.bias[half, side]
-        e = jnp.exp(s - jnp.max(s, axis=0, keepdims=True))
-        p = e * (1.0 / jnp.sum(e, axis=0, keepdims=True))
-        weights = p.astype(BF16)
-        dp = dot(v, g, NT)
-        delta = jnp.sum(p * dp, axis=0, keepdims=True)
-        ds = (p * (dp - delta)).astype(BF16)
-        place = pl.ds(pl.multiple_of(8 * j, 8), 16)
-        b.acc[pl.ds(frame, 14), place, :D] += dot(ds, q).reshape(14, 16, D)
-        b.acc[pl.ds(frame, 14), place, D:] += dot(weights, g).reshape(14, 16, D)
-        att = of_heads(dot(weights, v, TN))
-        dq = of_heads(dot(ds, k, TN)) * 0.125
-        return att.reshape(8, 8, D), dq.reshape(8, 8, D)
-
-    def tile_pair(i, carry):
-        one_pair(0, i)
-        one_pair(1, i)
-        return carry
-
-    def one_pair(half, jp):
-        a0, d0 = one_tile(half, 2 * jp, jnp.where(jp == 0, 0, 1))
-        a1, d1 = one_tile(half, 2 * jp + 1, jnp.where(jp == 7, 2, 1))
+    def some_tiles(tiles):
+        n = range(len(tiles))
+        k = [b.k_win[pl.ds(half * 8, 14), j].reshape(224, D) for half, j, side in tiles]
+        v = [b.v_win[pl.ds(half * 8, 14), j].reshape(224, D) for half, j, side in tiles]
+        q = [by_head(b.q_tiles[half, j]) for half, j, side in tiles]
+        g = [by_head(b.g_tiles[half, j]) for half, j, side in tiles]
+        s = [dot(k[i], q[i], NT) + b.bias[half, side] for i, (half, j, side) in enumerate(tiles)]
+        dp = [dot(v[i], g[i], NT) for i in n]
+        e = [jnp.exp(s[i] - jnp.max(s[i], axis=0, keepdims=True)) for i in n]
+        p = [e[i] * (1.0 / jnp.sum(e[i], axis=0, keepdims=True)) for i in n]
+        weights = [p[i].astype(BF16) for i in n]
+        for i, (half, j, side) in enumerate(tiles):
+            b.acc[pl.ds(half * 8, 14), pl.ds(pl.multiple_of(8 * j, 8), 16), D:] += dot(weights[i], g[i]).reshape(14, 16, D)
+        att = [of_heads(dot(weights[i], v[i], TN)).reshape(8, 8, D) for i in n]
+        delta = [jnp.sum(p[i] * dp[i], axis=0, keepdims=True) for i in n]
+        ds = [(p[i] * (dp[i] - delta[i])).astype(BF16) for i in n]
+        for i, (half, j, side) in enumerate(tiles):
+            b.acc[pl.ds(half * 8, 14), pl.ds(pl.multiple_of(8 * j, 8), 16), :D] += dot(ds[i], q[i]).reshape(14, 16, D)
+        dq = [(of_heads(dot(ds[i], k[i], TN)) * 0.125).reshape(8, 8, D) for i in n]
+        return att, dq
+
+    def store(half, jp, att, dq):
         cols = pl.ds(pl.multiple_of(16 * jp, 16), 16)
-        b.attended[pl.ds(half * 8, 8), cols, :] = jnp.concatenate([a0, a1], axis=1).astype(BF16)
-        b.joined[pl.ds(half * 8 + 3, 8), cols, :D] = jnp.concatenate([d0, d1], axis=1).astype(BF16)
-
-    lax.fori_loop(0, 8, tile_pair, 0)
+        b.attended[pl.ds(half * 8, 8), cols, :] = jnp.concatenate(att, axis=1).astype(BF16)
+        b.joined[pl.ds(half * 8 + 3, 8), cols, :D] = jnp.concatenate(dq, axis=1).astype(BF16)
+
+    def tile_pairs(jp, carry):
+        left, right = jnp.where(jp == 0, 0, 1), jnp.where(jp == 7, 2, 1)
+        att, dq = some_tiles([(half, 2 * jp + i, (left, right)[i]) for half in range(2) for i in range(2)])
+        for half in range(2):
+            store(half, jp, att[2 * half : 2 * half + 2], dq[2 * half : 2 * half + 2])
+        return carry
+
+    lax.fori_loop(0, 8, tile_pairs, 0)
 
 
 def weight_sums(b):

time: 62.5 us -> 58 us (0.928)
  Pallas kernels: 61.7 us -> 57.2 us
    pallas_call x1, Pallas kernels: 58.9 us -> 54.5 us  [block(): pl.pallas_call(kernel, out_shape=tuple((jax.ShapeDtypeStruct(*o) for o in...]
where the time goes in v5:
time: 58 us; the launch traced here: 57.9 us
  Pallas kernels  57.2 us (99%)
  between operations  0.64 us (1%)
    pallas_call x1, Pallas kernels, block(): pl.pallas_call(kernel, out_shape=tuple((jax.ShapeDtypeStruct(*o) for o in...  54.5 us
    pallas_call x1, Pallas kernels, outputs(): pl.pallas_call(kernel, out_shape=(jax.ShapeDtypeStruct((OWN, COLS, D), BF...  2.78 us

profile of v5, /device:TPU:1, one launch (start us, length us, event | category | flops | bytes accessed | tf_op | source)
XLA Modules:
  0.0 57.9 jit_solution(14467625325117205082)
XLA Ops:
  0.6 54.5 %shard_map.84 = (bf16[16,128,256]{2,1,0:T(8,128)(2,1)}, bf16[32,16,512]{2,1,0:T(8,128)(2,1)}) custom-call(bf16[16,128,256]{2,1,0:T(8,128)(2,1)} %bitcast.5, bf16[16,128,256]{2,1,0:T(8,128)(2,1)} %bitcast.6, f32[1,256]{1,0:T(1,128)} %bitcast.7, bf16[256,768]{1,0:T(8,128)(2,1)} %w_hbm.1, bf16[256,256]{1,0:T(8,128)(2,1)} %refs_4_.1), custom_call_target="tpu_custom_call" | custom-call | tf_op jit(solution)/shard_map/pallas_call | solution.py:414
  55.1 2.8 %shard_map.85 = (bf16[16,128,256]{2,1,0:T(8,128)(2,1)}, f32[256,768]{1,0:T(8,128)}, f32[256,256]{1,0:T(8,128)}, f32[1,256]{1,0:T(1,128)}) custom-call(bf16[16,128,256]{2,1,0:T(8,128)(2,1)} %get-tuple-element.10.gt_hbm, bf16[32,16,512]{2,1,0:T(8,128)(2,1)} %get-tuple-element.11.full_hbm, f32[1,256]{1,0:T(1,128)} %bitcast.8, bf16[256,768]{1,0:T(8,128)(2,1)} %w_hbm.1), custom_call_target="tpu_custom_call" | custom-call | tf_op jit(solution)/shard_map/pallas_call | solution.py:469

commit v6 on v5

--- a/solution.py
+++ b/solution.py
@@ -16,6 +16,8 @@
 FRAME = OWN + 6
 PADDED = 144
 NEG = -1e30
+KEYS = 160
+LANES = 128
 NT = (((1,), (1,)), ((), ()))
 TN = (((0,), (0,)), ((), ()))
 VMEM_BYTES = 58 * 1024 * 1024
@@ -30,7 +32,7 @@
     "g_tiles": ((2, 16, 64, D), BF16),
     "attended": ((OWN, COLS, D), BF16),
     "joined": ((FRAME, COLS, 3 * D), BF16),
-    "bias": ((2, 3, 224, D), F32),
+    "bias": ((3, 3, KEYS, LANES), F32),
     "acc": ((FRAME, PADDED, 2 * D), F32),
     "gn": ((OWN, COLS, D), F32),
     "sums": ((32, 16, 512), BF16),
@@ -72,23 +74,15 @@
 
 
 def mask(b, here, last):
-    key = lax.broadcasted_iota(jnp.int32, (224, D), 0)
-    lane = lax.broadcasted_iota(jnp.int32, (224, D), 1)
+    key = lax.broadcasted_iota(jnp.int32, (KEYS, LANES), 0)
+    lane = lax.broadcasted_iota(jnp.int32, (KEYS, LANES), 1)
     k_row, k_col = key // 16, key % 16
-    q_row, q_col = (lane % 64) // 8, lane % 8
+    q_row, q_col = (lane % 32) // 8, lane % 8
     near = (k_row - q_row >= 0) & (k_row - q_row <= 6) & (k_col - q_col >= 1) & (k_col - q_col <= 7)
-    for half in range(2):
-        if half == 0:
-            inside = near & ((k_row >= 3) | (here > 0))
-        else:
-            inside = near & ((k_row < 11) | (here < last))
-        for side in range(3):
-            ok = inside
-            if side == 0:
-                ok = ok & (k_col >= 4)
-            if side == 2:
-                ok = ok & (k_col < 12)
-            b.bias[half, side] = jnp.where(ok, 0.0, NEG)
+    inside = (near & ((k_row >= 3) | (here > 0)), near, near & ((k_row < 7) | (here < last)))
+    for rows in range(3):
+        for side, ok in enumerate((k_col >= 4, k_col >= 0, k_col < 12)):
+            b.bias[rows, side] = jnp.where(inside[rows] & ok, 0.0, NEG)
 
 
 def own_rows(b):
@@ -126,53 +120,57 @@
 
 
 def attend(b):
-    head_lane = lax.broadcasted_iota(jnp.int32, (64, D), 1) // 64
-
-    def by_head(tile):
+    head_lane = lax.broadcasted_iota(jnp.int32, (32, D), 1) // 64
+
+    def by_head(source, tile):
+        band, j, side = tile
+        rows = source[band // 2, j, 32 * (band % 2) : 32 * (band % 2) + 32]
         return jnp.concatenate(
-            [jnp.where(head_lane == h, tile, jnp.zeros_like(tile)) for h in range(4)], axis=0
+            [jnp.where(head_lane == h, rows, jnp.zeros_like(rows)) for h in range(4)], axis=0
         )
 
     def of_heads(full):
-        out = full[192:256]
+        out = full[96:128]
         for h in (2, 1, 0):
-            out = jnp.where(head_lane == h, full[64 * h : 64 * h + 64], out)
-        return out
+            out = jnp.where(head_lane == h, full[32 * h : 32 * h + 32], out)
+        return out.reshape(4, 8, D)
+
+    def add(tile, lanes, term):
+        band, j, side = tile
+        b.acc[4 * band : 4 * band + 10, pl.ds(pl.multiple_of(8 * j, 8), 16), lanes] += term.reshape(10, 16, D)
 
     def some_tiles(tiles):
         n = range(len(tiles))
-        k = [b.k_win[pl.ds(half * 8, 14), j].reshape(224, D) for half, j, side in tiles]
-        v = [b.v_win[pl.ds(half * 8, 14), j].reshape(224, D) for half, j, side in tiles]
-        q = [by_head(b.q_tiles[half, j]) for half, j, side in tiles]
-        g = [by_head(b.g_tiles[half, j]) for half, j, side in tiles]
-        s = [dot(k[i], q[i], NT) + b.bias[half, side] for i, (half, j, side) in enumerate(tiles)]
+        k = [b.k_win[4 * band : 4 * band + 10, j].reshape(KEYS, D) for band, j, side in tiles]
+        v = [b.v_win[4 * band : 4 * band + 10, j].reshape(KEYS, D) for band, j, side in tiles]
+        q = [by_head(b.q_tiles, tile) for tile in tiles]
+        g = [by_head(b.g_tiles, tile) for tile in tiles]
+        s = [dot(k[i], q[i], NT) + b.bias[(0, 1, 1, 2)[u[0]], u[2]] for i, u in enumerate(tiles)]
         dp = [dot(v[i], g[i], NT) for i in n]
         e = [jnp.exp(s[i] - jnp.max(s[i], axis=0, keepdims=True)) for i in n]
         p = [e[i] * (1.0 / jnp.sum(e[i], axis=0, keepdims=True)) for i in n]
         weights = [p[i].astype(BF16) for i in n]
-        for i, (half, j, side) in enumerate(tiles):
-            b.acc[pl.ds(half * 8, 14), pl.ds(pl.multiple_of(8 * j, 8), 16), D:] += dot(weights[i], g[i]).reshape(14, 16, D)
-        att = [of_heads(dot(weights[i], v[i], TN)).reshape(8, 8, D) for i in n]
+        for i, u in enumerate(tiles):
+            add(u, slice(D, 2 * D), dot(weights[i], g[i]))
+        att = [of_heads(dot(weights[i], v[i], TN)) for i in n]
         delta = [jnp.sum(p[i] * dp[i], axis=0, keepdims=True) for i in n]
         ds = [(p[i] * (dp[i] - delta[i])).astype(BF16) for i in n]
-        for i, (half, j, side) in enumerate(tiles):
-            b.acc[pl.ds(half * 8, 14), pl.ds(pl.multiple_of(8 * j, 8), 16), :D] += dot(ds[i], q[i]).reshape(14, 16, D)
-        dq = [(of_heads(dot(ds[i], k[i], TN)) * 0.125).reshape(8, 8, D) for i in n]
-        return att, dq
-
-    def store(half, jp, att, dq):
-        cols = pl.ds(pl.multiple_of(16 * jp, 16), 16)
-        b.attended[pl.ds(half * 8, 8), cols, :] = jnp.concatenate(att, axis=1).astype(BF16)
-        b.joined[pl.ds(half * 8 + 3, 8), cols, :D] = jnp.concatenate(dq, axis=1).astype(BF16)
-
-    def tile_pairs(jp, carry):
-        left, right = jnp.where(jp == 0, 0, 1), jnp.where(jp == 7, 2, 1)
-        att, dq = some_tiles([(half, 2 * jp + i, (left, right)[i]) for half in range(2) for i in range(2)])
-        for half in range(2):
-            store(half, jp, att[2 * half : 2 * half + 2], dq[2 * half : 2 * half + 2])
-        return carry
-
-    lax.fori_loop(0, 8, tile_pairs, 0)
+        for i, u in enumerate(tiles):
+            add(u, slice(0, D), dot(ds[i], q[i]))
+        dq = [of_heads(dot(ds[i], k[i], TN)) * 0.125 for i in n]
+        for i in range(0, len(tiles), 2):
+            band, j, side = tiles[i]
+            cols = pl.ds(pl.multiple_of(8 * j, 16), 16)
+            b.attended[4 * band : 4 * band + 4, cols, :] = jnp.concatenate(att[i : i + 2], axis=1).astype(BF16)
+            b.joined[4 * band + 3 : 4 * band + 7, cols, :D] = jnp.concatenate(dq[i : i + 2], axis=1).astype(BF16)
+
+    def columns(jp, carry):
+        sides = jnp.where(jp == 0, 0, 1), jnp.where(jp == 7, 2, 1)
+        tiles = [(band, 2 * jp + i, sides[i]) for band in range(4) for i in range(2)]
+        some_tiles(tiles)
+        return carry
+
+    lax.fori_loop(0, 8, columns, 0)
 
 
 def weight_sums(b):
@@ -272,13 +270,21 @@
     greet(partner)
     lax.fori_loop(1, 16, greet_plane, 0)
     lax.fori_loop(1, 8, greet_z, 0)
+    loads = [
+        pltpu.make_async_copy(src, dst, b.load.at[i])
+        for i, (src, dst) in enumerate(
+            ((b.tok_hbm, b.tok), (b.w_in_hbm, b.w_in), (b.gain_hbm, b.gain), (b.w_out_hbm, b.w_out), (b.cot_hbm, b.cot))
+        )
+    ]
+    for copy in loads:
+        copy.start()
     clear(b)
     pl.semaphore_wait(barrier, 25)
 
     def halo_copies():
         return (
-            remote(b.tok.at[pl.ds(OWN - 3, 3)], b.halo.at[0], b.near_send.at[0], b.near_recv.at[0], after),
-            remote(b.tok.at[pl.ds(0, 3)], b.halo.at[1], b.near_send.at[1], b.near_recv.at[1], before),
+            remote(b.tok_hbm.at[pl.ds(OWN - 3, 3)], b.halo.at[0], b.near_send.at[0], b.near_recv.at[0], after),
+            remote(b.tok_hbm.at[pl.ds(0, 3)], b.halo.at[1], b.near_send.at[1], b.near_recv.at[1], before),
         )
 
     def rim_copies():
@@ -326,12 +332,18 @@
     for copy in halo_copies():
         copy.start()
     mask(b, rows, count - 1)
+    for copy in loads:
+        copy.wait()
     own_rows(b)
     for copy in halo_copies():
         copy.wait_recv()
     halo_rows(b)
     attend(b)
     weight_sums(b)
+    stores = [
+        pltpu.make_async_copy(b.gt.at[pl.ds(low, n)], b.gt_hbm.at[pl.ds(low, n)], b.store.at[i])
+        for i, (low, n) in enumerate(((3, 10), (0, 3), (OWN - 3, 3)))
+    ]
     each(core_scatter, 1, 16, start)
     core_scatter(0).start()
     rim_rows(b)
@@ -358,6 +370,7 @@
     b.z_all[z] = total.astype(BF16)
     each(z_share, 1, 8, start)
     finish_rows(b, 3, 13)
+    stores[0].start()
     each(z_share, 1, 8, wait_recv)
     whole = b.z_all[0].astype(F32)
     for i in range(1, 8):
@@ -374,6 +387,8 @@
         return carry
 
     lax.fori_loop(0, 3, edge, 0)
+    stores[1].start()
+    stores[2].start()
 
     def pass_on(i, carry):
         gather(i).wait_recv()
@@ -384,6 +399,8 @@
     each(core_gather, 0, 16, wait_recv)
     for copy in halo_copies() + rim_copies():
         copy.wait_send()
+    for copy in stores:
+        copy.wait()
     each(core_scatter, 0, 16, wait_send)
     each(scatter, 1, 16, wait_send)
     each(z_share, 1, 8, wait_send)
@@ -392,21 +409,27 @@
 
 
 def block(tok, cot, gain, w_in, w_out):
-    vmem = pl.BlockSpec(memory_space=pltpu.VMEM)
+    vmem, hbm = pl.BlockSpec(memory_space=pltpu.VMEM), pl.BlockSpec(memory_space=pltpu.HBM)
     dma = pltpu.SemaphoreType.DMA
-    outs = {"gt": ((OWN, COLS, D), BF16), "full": ((32, 16, 512), BF16)}
+    outs = {"gt_hbm": ((OWN, COLS, D), BF16), "full": ((32, 16, 512), BF16)}
     slots = {
+        "tok": ((OWN, COLS, D), BF16),
+        "cot": ((OWN, COLS, D), BF16),
+        "gain": ((1, D), F32),
+        "w_in": ((D, 3 * D), BF16),
+        "w_out": ((D, D), BF16),
+        "gt": ((OWN, COLS, D), BF16),
         "core_got": ((16, 16, 512), BF16),
         "paired": ((16, 16, 512), BF16),
         "plane_got": ((16, 16, 512), BF16),
         "z_all": ((8, 16, 512), BF16),
     }
     sems = {
-        "near_send": 4, "near_recv": 4, "core_send": 16, "core_recv": 16, "plane_send": 16, "plane_recv": 16,
+        "load": 5, "store": 3, "near_send": 4, "near_recv": 4, "core_send": 16, "core_recv": 16, "plane_send": 16, "plane_recv": 16,
         "z_send": 8, "z_recv": 8, "out_send": 16, "out_recv": 16,
         "last_send": 16, "last_recv": 16,
     }
-    names = ["tok", "cot", "gain", "w_in", "w_out", *outs, *BUFFERS, *slots, *sems]
+    names = ["tok_hbm", "cot_hbm", "gain_hbm", "w_in_hbm", "w_out_hbm", *outs, *BUFFERS, *slots, *sems]
 
     def kernel(*refs):
         block_kernel(names, *refs)
@@ -414,8 +437,8 @@
     return pl.pallas_call(
         kernel,
         out_shape=tuple(jax.ShapeDtypeStruct(*o) for o in outs.values()),
-        in_specs=[vmem] * 5,
-        out_specs=(vmem,) * 2,
+        in_specs=[hbm] * 5,
+        out_specs=(hbm, vmem),
         scratch_shapes=[
             *(pltpu.VMEM(*s) for s in BUFFERS.values()),
             *(pltpu.VMEM(*s) for s in slots.values()),

time: 58 us -> 55.8 us (0.962)
  Pallas kernels: 57.2 us -> 55.1 us
    pallas_call x1, Pallas kernels: 54.5 us -> 52.3 us  [block(): pl.pallas_call(kernel, out_shape=tuple((jax.ShapeDtypeStruct(*o) for o in...]
where the time goes in v6:
time: 55.8 us; the launch traced here: 55.7 us
  Pallas kernels  55.1 us (99%)
  between operations  0.64 us (1%)
    pallas_call x1, Pallas kernels, block(): pl.pallas_call(kernel, out_shape=tuple((jax.ShapeDtypeStruct(*o) for o in...  52.3 us
    pallas_call x1, Pallas kernels, outputs(): pl.pallas_call(kernel, out_shape=(jax.ShapeDtypeStruct((OWN, COLS, D), BF...  2.78 us

profile of v6, /device:TPU:1, one launch (start us, length us, event | category | flops | bytes accessed | tf_op | source)
XLA Modules:
  0.0 55.7 jit_solution(11510721032800256715)
XLA Ops:
  0.6 52.3 %shard_map.84 = (bf16[16,128,256]{2,1,0:T(8,128)(2,1)}, bf16[32,16,512]{2,1,0:T(8,128)(2,1)}) custom-call(bf16[16,128,256]{2,1,0:T(8,128)(2,1)} %bitcast.5, bf16[16,128,256]{2,1,0:T(8,128)(2,1)} %bitcast.6, f32[1,256]{1,0:T(1,128)} %bitcast.7, bf16[256,768]{1,0:T(8,128)(2,1)} %w_hbm.1, bf16[256,256]{1,0:T(8,128)(2,1)} %refs_4_.1), custom_call_target="tpu_custom_call" | custom-call | tf_op jit(solution)/shard_map/pallas_call | solution.py:437
  52.9 2.8 %shard_map.85 = (bf16[16,128,256]{2,1,0:T(8,128)(2,1)}, f32[256,768]{1,0:T(8,128)}, f32[256,256]{1,0:T(8,128)}, f32[1,256]{1,0:T(1,128)}) custom-call(bf16[16,128,256]{2,1,0:T(8,128)(2,1)} %get-tuple-element.10.gt_hbm, bf16[32,16,512]{2,1,0:T(8,128)(2,1)} %get-tuple-element.11.full_hbm, f32[1,256]{1,0:T(1,128)} %bitcast.8, bf16[256,768]{1,0:T(8,128)(2,1)} %w_hbm.1), custom_call_target="tpu_custom_call" | custom-call | tf_op jit(solution)/shard_map/pallas_call | solution.py:492

commit v7 on v6

--- a/solution.py
+++ b/solution.py
@@ -116,7 +116,8 @@
         windows(b, b.halo[1, r], 1, OWN + 3 + r)
         return carry
 
-    lax.fori_loop(0, 3, halo_row, 0)
+    for r in range(3):
+        halo_row(r, 0)
 
 
 def attend(b):
@@ -150,14 +151,14 @@
         e = [jnp.exp(s[i] - jnp.max(s[i], axis=0, keepdims=True)) for i in n]
         p = [e[i] * (1.0 / jnp.sum(e[i], axis=0, keepdims=True)) for i in n]
         weights = [p[i].astype(BF16) for i in n]
+        delta = [jnp.sum(p[i] * dp[i], axis=0, keepdims=True) for i in n]
+        ds = [(p[i] * (dp[i] - delta[i])).astype(BF16) for i in n]
+        att = [of_heads(dot(weights[i], v[i], TN)) for i in n]
+        dq = [of_heads(dot(ds[i], k[i], TN)) * 0.125 for i in n]
         for i, u in enumerate(tiles):
             add(u, slice(D, 2 * D), dot(weights[i], g[i]))
-        att = [of_heads(dot(weights[i], v[i], TN)) for i in n]
-        delta = [jnp.sum(p[i] * dp[i], axis=0, keepdims=True) for i in n]
-        ds = [(p[i] * (dp[i] - delta[i])).astype(BF16) for i in n]
         for i, u in enumerate(tiles):
             add(u, slice(0, D), dot(ds[i], q[i]))
-        dq = [of_heads(dot(ds[i], k[i], TN)) * 0.125 for i in n]
         for i in range(0, len(tiles), 2):
             band, j, side = tiles[i]
             cols = pl.ds(pl.multiple_of(8 * j, 16), 16)
@@ -173,18 +174,22 @@
     lax.fori_loop(0, 8, columns, 0)
 
 
-def weight_sums(b):
+def round_keys(b):
     def key_row(r, carry):
         b.joined[r, :, D:] = b.acc[r, 4 : 4 + COLS, :].astype(BF16)
         return carry
 
-    lax.fori_loop(0, FRAME, key_row, 0)
-    g_in = dot(b.normed[...].reshape(FRAME * COLS, D), b.joined[...].reshape(FRAME * COLS, 3 * D), TN)
-    g_out = dot(b.attended[...].reshape(OWN * COLS, D), b.cot[...].reshape(OWN * COLS, D), TN)
-    for g in range(16):
+    lax.fori_loop(0, FRAME, key_row, 0, unroll=True)
+
+
+def weight_sums(b, part):
+    lanes = pl.ds(pl.multiple_of(128 * part, 128), 128)
+    g_in = dot(b.normed[:, :, lanes].reshape(FRAME * COLS, 128), b.joined[...].reshape(FRAME * COLS, 3 * D), TN)
+    g_out = dot(b.attended[:, :, lanes].reshape(OWN * COLS, 128), b.cot[...].reshape(OWN * COLS, D), TN)
+    for g in range(8):
         span = slice(16 * g, 16 * g + 16)
-        b.sums[2 * g] = g_in[span, :512].astype(BF16)
-        b.sums[2 * g + 1] = jnp.concatenate([g_in[span, 512:], g_out[span]], axis=1).astype(BF16)
+        b.sums[16 * part + 2 * g] = g_in[span, :512].astype(BF16)
+        b.sums[16 * part + 2 * g + 1] = jnp.concatenate([g_in[span, 512:], g_out[span]], axis=1).astype(BF16)
 
 
 def rim_rows(b):
@@ -236,15 +241,25 @@
     mine = 16 * core
     other = 16 - mine
 
+    def away(i):
+        return i + i // 2 - 2 * (i // 3)
+
+    def offsets(i):
+        n = (16 - i) % 16
+        return away(n // 4), away(n % 4)
+
     def in_plane(i):
-        to_y, to_x = (y + i // 4) % 4, (x + i % 4) % 4
+        by_y, by_x = offsets(i)
+        to_y, to_x = (y + by_y) % 4, (x + by_x) % 4
         return {"rows": (to_y * 8 + z) * 2 + core, "dp": to_x}, to_y * 4 + to_x
 
     def from_plane(i):
-        return ((y + 4 - i // 4) % 4) * 4 + (x + 4 - i % 4) % 4
+        by_y, by_x = offsets(i)
+        return ((y + 4 - by_y) % 4) * 4 + (x + 4 - by_x) % 4
 
     def along_z(i):
-        return {"rows": (y * 8 + (z + i) % 8) * 2 + core, "dp": x}
+        by_z = 4 + (i // 2) * (2 * (i % 2) - 1)
+        return {"rows": (y * 8 + (z + by_z) % 8) * 2 + core, "dp": x}
 
     def remote(src, dst, send, recv, where):
         return pltpu.make_async_remote_copy(
@@ -339,13 +354,15 @@
         copy.wait_recv()
     halo_rows(b)
     attend(b)
-    weight_sums(b)
+    round_keys(b)
+    weight_sums(b, 1 - core)
     stores = [
         pltpu.make_async_copy(b.gt.at[pl.ds(low, n)], b.gt_hbm.at[pl.ds(low, n)], b.store.at[i])
         for i, (low, n) in enumerate(((3, 10), (0, 3), (OWN - 3, 3)))
     ]
     each(core_scatter, 1, 16, start)
     core_scatter(0).start()
+    weight_sums(b, core)
     rim_rows(b)
     for copy in rim_copies():
         copy.start()
@@ -391,8 +408,8 @@
     stores[2].start()
 
     def pass_on(i, carry):
-        gather(i).wait_recv()
-        core_gather(i).start()
+        gather(16 - i).wait_recv()
+        core_gather(16 - i).start()
         return carry
 
     lax.fori_loop(1, 16, pass_on, 0)

time: 55.8 us -> 54.2 us (0.971)
  Pallas kernels: 55.1 us -> 53.4 us
    pallas_call x1, Pallas kernels: 52.3 us -> 50.6 us  [block(): pl.pallas_call(kernel, out_shape=tuple((jax.ShapeDtypeStruct(*o) for o in...]
where the time goes in v7:
time: 54.2 us; the launch traced here: 54.1 us
  Pallas kernels  53.4 us (99%)
  between operations  0.64 us (1%)
    pallas_call x1, Pallas kernels, block(): pl.pallas_call(kernel, out_shape=tuple((jax.ShapeDtypeStruct(*o) for o in...  50.6 us
    pallas_call x1, Pallas kernels, outputs(): pl.pallas_call(kernel, out_shape=(jax.ShapeDtypeStruct((OWN, COLS, D), BF...  2.78 us

profile of v7, /device:TPU:1, one launch (start us, length us, event | category | flops | bytes accessed | tf_op | source)
XLA Modules:
  0.0 54.1 jit_solution(2231185982580325307)
XLA Ops:
  0.6 50.6 %shard_map.84 = (bf16[16,128,256]{2,1,0:T(8,128)(2,1)}, bf16[32,16,512]{2,1,0:T(8,128)(2,1)}) custom-call(bf16[16,128,256]{2,1,0:T(8,128)(2,1)} %bitcast.5, bf16[16,128,256]{2,1,0:T(8,128)(2,1)} %bitcast.6, f32[1,256]{1,0:T(1,128)} %bitcast.7, bf16[256,768]{1,0:T(8,128)(2,1)} %w_hbm.1, bf16[256,256]{1,0:T(8,128)(2,1)} %refs_4_.1), custom_call_target="tpu_custom_call" | custom-call | tf_op jit(solution)/shard_map/pallas_call | solution.py:454
  51.3 2.8 %shard_map.85 = (bf16[16,128,256]{2,1,0:T(8,128)(2,1)}, f32[256,768]{1,0:T(8,128)}, f32[256,256]{1,0:T(8,128)}, f32[1,256]{1,0:T(1,128)}) custom-call(bf16[16,128,256]{2,1,0:T(8,128)(2,1)} %get-tuple-element.10.gt_hbm, bf16[32,16,512]{2,1,0:T(8,128)(2,1)} %get-tuple-element.11.full_hbm, f32[1,256]{1,0:T(1,128)} %bitcast.8, bf16[256,768]{1,0:T(8,128)(2,1)} %w_hbm.1), custom_call_target="tpu_custom_call" | custom-call | tf_op jit(solution)/shard_map/pallas_call | solution.py:509

commit v8 on v7

--- a/solution.py
+++ b/solution.py
@@ -171,7 +171,7 @@
         some_tiles(tiles)
         return carry
 
-    lax.fori_loop(0, 8, columns, 0)
+    lax.fori_loop(0, 8, columns, 0, unroll=2)
 
 
 def round_keys(b):
@@ -267,24 +267,6 @@
             device_id=where, device_id_type=pl.DeviceIdType.MESH,
         )
 
-    barrier = pltpu.get_barrier_semaphore()
-
-    def greet(where):
-        pl.semaphore_signal(barrier, inc=1, device_id=where, device_id_type=pl.DeviceIdType.MESH)
-
-    def greet_plane(i, carry):
-        greet(in_plane(i)[0])
-        return carry
-
-    def greet_z(i, carry):
-        greet(along_z(i))
-        return carry
-
-    greet(before)
-    greet(after)
-    greet(partner)
-    lax.fori_loop(1, 16, greet_plane, 0)
-    lax.fori_loop(1, 8, greet_z, 0)
     loads = [
         pltpu.make_async_copy(src, dst, b.load.at[i])
         for i, (src, dst) in enumerate(
@@ -293,7 +275,24 @@
     ]
     for copy in loads:
         copy.start()
-    clear(b)
+    barrier = pltpu.get_barrier_semaphore()
+
+    def greet(where):
+        pl.semaphore_signal(barrier, inc=1, device_id=where, device_id_type=pl.DeviceIdType.MESH)
+
+    def greet_plane(i, carry):
+        greet(in_plane(i)[0])
+        return carry
+
+    def greet_z(i, carry):
+        greet(along_z(i))
+        return carry
+
+    greet(before)
+    greet(after)
+    greet(partner)
+    lax.fori_loop(1, 16, greet_plane, 0)
+    lax.fori_loop(1, 8, greet_z, 0)
     pl.semaphore_wait(barrier, 25)
 
     def halo_copies():
@@ -346,6 +345,7 @@
 
     for copy in halo_copies():
         copy.start()
+    clear(b)
     mask(b, rows, count - 1)
     for copy in loads:
         copy.wait()
@@ -406,6 +406,11 @@
     lax.fori_loop(0, 3, edge, 0)
     stores[1].start()
     stores[2].start()
+    for copy in halo_copies() + rim_copies():
+        copy.wait_send()
+    each(core_scatter, 0, 16, wait_send)
+    each(scatter, 1, 16, wait_send)
+    each(z_share, 1, 8, wait_send)
 
     def pass_on(i, carry):
         gather(16 - i).wait_recv()
@@ -414,13 +419,8 @@
 
     lax.fori_loop(1, 16, pass_on, 0)
     each(core_gather, 0, 16, wait_recv)
-    for copy in halo_copies() + rim_copies():
-        copy.wait_send()
     for copy in stores:
         copy.wait()
-    each(core_scatter, 0, 16, wait_send)
-    each(scatter, 1, 16, wait_send)
-    each(z_share, 1, 8, wait_send)
     each(gather, 1, 16, wait_send)
     each(core_gather, 0, 16, wait_send)
 

time: 54.2 us -> 53.5 us (0.987)
  Pallas kernels: 53.4 us -> 52.8 us
    pallas_call x1, Pallas kernels: 50.6 us -> 50 us  [block(): pl.pallas_call(kernel, out_shape=tuple((jax.ShapeDtypeStruct(*o) for o in...]
where the time goes in v8:
time: 53.5 us; the launch traced here: 53.4 us
  Pallas kernels  52.8 us (99%)
  between operations  0.64 us (1%)
    pallas_call x1, Pallas kernels, block(): pl.pallas_call(kernel, out_shape=tuple((jax.ShapeDtypeStruct(*o) for o in...  50 us
    pallas_call x1, Pallas kernels, outputs(): pl.pallas_call(kernel, out_shape=(jax.ShapeDtypeStruct((OWN, COLS, D), BF...  2.78 us

profile of v8, /device:TPU:1, one launch (start us, length us, event | category | flops | bytes accessed | tf_op | source)
XLA Modules:
  0.0 53.4 jit_solution(7125885030346313430)
XLA Ops:
  0.6 50.0 %shard_map.84 = (bf16[16,128,256]{2,1,0:T(8,128)(2,1)}, bf16[32,16,512]{2,1,0:T(8,128)(2,1)}) custom-call(bf16[16,128,256]{2,1,0:T(8,128)(2,1)} %bitcast.5, bf16[16,128,256]{2,1,0:T(8,128)(2,1)} %bitcast.6, f32[1,256]{1,0:T(1,128)} %bitcast.7, bf16[256,768]{1,0:T(8,128)(2,1)} %w_hbm.1, bf16[256,256]{1,0:T(8,128)(2,1)} %refs_4_.1), custom_call_target="tpu_custom_call" | custom-call | tf_op jit(solution)/shard_map/pallas_call | solution.py:454
  50.7 2.8 %shard_map.85 = (bf16[16,128,256]{2,1,0:T(8,128)(2,1)}, f32[256,768]{1,0:T(8,128)}, f32[256,256]{1,0:T(8,128)}, f32[1,256]{1,0:T(1,128)}) custom-call(bf16[16,128,256]{2,1,0:T(8,128)(2,1)} %get-tuple-element.10.gt_hbm, bf16[32,16,512]{2,1,0:T(8,128)(2,1)} %get-tuple-element.11.full_hbm, f32[1,256]{1,0:T(1,128)} %bitcast.8, bf16[256,768]{1,0:T(8,128)(2,1)} %w_hbm.1), custom_call_target="tpu_custom_call" | custom-call | tf_op jit(solution)/shard_map/pallas_call | solution.py:509

commit v9 on v8

--- a/solution.py
+++ b/solution.py
@@ -171,7 +171,7 @@
         some_tiles(tiles)
         return carry
 
-    lax.fori_loop(0, 8, columns, 0, unroll=2)
+    lax.fori_loop(0, 8, columns, 0, unroll=4)
 
 
 def round_keys(b):
@@ -485,6 +485,7 @@
         gain_write = pltpu.make_async_copy(g_gain, g_gain_out, sem.at[22])
         for copy in parts + small + reads:
             copy.start()
+        per_row = []
         for i in range(4):
             parts[i].wait()
             for g in range(4 * i, 4 * i + 4):
@@ -497,10 +498,14 @@
             out_writes[i].start()
             reads[i].wait()
             writes[i].start()
-        for copy in small:
-            copy.wait()
-        per_row = jnp.sum(g_in[...] * w[...].astype(F32), axis=1, keepdims=True)
-        g_gain[...] = jnp.transpose(jnp.broadcast_to(per_row, (D, 128)))[0:1] / gain_ref[...]
+            if i == 0:
+                for copy in small:
+                    copy.wait()
+            rows_here = slice(64 * i, 64 * i + 64)
+            term = g_in[rows_here, :] * w[rows_here, :].astype(F32)
+            per_row.append(jnp.sum(term, axis=1, keepdims=True))
+        column = jnp.broadcast_to(jnp.concatenate(per_row, axis=0), (D, 128))
+        g_gain[...] = jnp.transpose(column)[0:1] / gain_ref[...]
         gain_write.start()
         for copy in writes + in_writes + out_writes + [gain_write]:
             copy.wait()

time: 53.5 us -> 53.3 us (level)
  no operation moved by 1% of the time
where the time goes in v9:
time: 53.3 us; the launch traced here: 53.2 us
  Pallas kernels  52.6 us (99%)
  between operations  0.64 us (1%)
    pallas_call x1, Pallas kernels, block(): pl.pallas_call(kernel, out_shape=tuple((jax.ShapeDtypeStruct(*o) for o in...  49.8 us
    pallas_call x1, Pallas kernels, outputs(): pl.pallas_call(kernel, out_shape=(jax.ShapeDtypeStruct((OWN, COLS, D), BF...  2.81 us

profile of v9, /device:TPU:1, one launch (start us, length us, event | category | flops | bytes accessed | tf_op | source)
XLA Modules:
  0.0 53.2 jit_solution(17533486443930607908)
XLA Ops:
  0.6 49.8 %shard_map.84 = (bf16[16,128,256]{2,1,0:T(8,128)(2,1)}, bf16[32,16,512]{2,1,0:T(8,128)(2,1)}) custom-call(bf16[16,128,256]{2,1,0:T(8,128)(2,1)} %bitcast.5, bf16[16,128,256]{2,1,0:T(8,128)(2,1)} %bitcast.6, f32[1,256]{1,0:T(1,128)} %bitcast.7, bf16[256,768]{1,0:T(8,128)(2,1)} %w_hbm.1, bf16[256,256]{1,0:T(8,128)(2,1)} %refs_4_.1), custom_call_target="tpu_custom_call" | custom-call | tf_op jit(solution)/shard_map/pallas_call | solution.py:454
  50.4 2.8 %shard_map.85 = (bf16[16,128,256]{2,1,0:T(8,128)(2,1)}, f32[256,768]{1,0:T(8,128)}, f32[256,256]{1,0:T(8,128)}, f32[1,256]{1,0:T(1,128)}) custom-call(bf16[16,128,256]{2,1,0:T(8,128)(2,1)} %get-tuple-element.10.gt_hbm, bf16[32,16,512]{2,1,0:T(8,128)(2,1)} %get-tuple-element.11.full_hbm, f32[1,256]{1,0:T(1,128)} %bitcast.8, bf16[256,768]{1,0:T(8,128)(2,1)} %w_hbm.1), custom_call_target="tpu_custom_call" | custom-call | tf_op jit(solution)/shard_map/pallas_call | solution.py:514
